TPU v7x, 128 devices: a whole 4x4x4 slice. The times are simulated.
128 devices in a mesh: seq: 8 (over z, y_hi), tensor: 16 (over y_lo, x, core).
Axes of the slice: x: 4, y: 4 (y_hi: 2, y_lo: 2; y = y_hi * 2 + y_lo), z: 4, core: 2. Of those that a mesh axis runs over, the one named last changes fastest.
Arguments:
- queries: bfloat16 [4096, 6144], P('seq', 'tensor'), may hold values from -120 to 120
- keys: bfloat16 [4096, 6144], P('seq', 'tensor'), may hold values from -4 to 4
- values: bfloat16 [4096, 6144], P('seq', 'tensor'), may hold values from -6 to 6
- stream: bfloat16 [4096, 6144], P('seq', 'tensor'), may hold values from -160 to 160
- out_weight: bfloat16 [6144, 6144], P('tensor'), may hold values from -0.109375 to 0.109375
- norm_gain: float32 [6144], replicated, may hold values from 0.5 to 1.5
- up_weight: bfloat16 [6144, 12288], P('seq', 'tensor'), may hold values from -0.078125 to 0.078125
Outputs:
- residual_out: bfloat16 [4096, 6144], P('seq', 'tensor')
- expanded: bfloat16 [4096, 12288], P('seq', 'tensor')
All inputs are finite; a program needn't handle non-finite values.
Results may differ from a plain program's by a relative error of at most 0.018.
Values may be sent and summed in bfloat16 or wider, within the bound.
A program may use at most 128 MiB of HBM per device.

v0:
```python
import math

import jax
import jax.numpy as jnp
from jax import lax
from jax.sharding import PartitionSpec as P

D = 6144
HD = 128


def body(queries, keys, values, stream, out_weight, norm_gain, up_weight):
    rows_here = queries.shape[0]
    heads_here = queries.shape[1] // HD
    softmax_scale = 1.0 / math.sqrt(HD)
    query_heads = queries.reshape(rows_here, heads_here, HD)
    running_max = jnp.full((heads_here, rows_here), -jnp.inf, jnp.float32)
    running_sum = jnp.zeros((heads_here, rows_here), jnp.float32)
    running_acc = jnp.zeros((heads_here, rows_here, HD), jnp.float32)
    key_piece = lax.all_gather(keys, "seq", axis=0, tiled=True)
    value_piece = lax.all_gather(values, "seq", axis=0, tiled=True)
    key_count = key_piece.shape[0]
    key_heads = key_piece.reshape(key_count, heads_here, HD)
    value_heads = value_piece.reshape(key_count, heads_here, HD)
    scores = (
        jnp.einsum("thd,shd->hts", query_heads, key_heads, preferred_element_type=jnp.float32)
        * softmax_scale
    )
    new_max = jnp.max(scores, axis=2)
    weights = jnp.exp(scores - new_max[:, :, None])
    decay_old = jnp.exp(running_max - new_max)
    new_sum = running_sum * decay_old + jnp.sum(weights, axis=2)
    gathered_values = jnp.einsum(
        "hts,shd->htd",
        weights.astype(jnp.bfloat16),
        value_heads,
        preferred_element_type=jnp.float32,
    )
    new_acc = running_acc * decay_old[:, :, None] + gathered_values
    attended = (new_acc / new_sum[:, :, None]).astype(jnp.bfloat16)
    attended = attended.transpose(1, 0, 2).reshape(rows_here, heads_here * HD)
    width_here = stream.shape[1]
    columns = out_weight
    mixed = lax.psum_scatter(
        lax.dot_general(
            columns, attended, (((0,), (1,)), ((), ())), preferred_element_type=jnp.float32
        ).astype(jnp.bfloat16),
        "tensor",
        scatter_dimension=0,
        tiled=True,
    ).astype(jnp.float32)
    residual_out = (stream.astype(jnp.float32) + mixed.T).astype(jnp.bfloat16)
    level = residual_out.astype(jnp.float32)
    partial_squares = jnp.sum(level * level, axis=1)
    square_total = lax.psum(partial_squares, "tensor")
    inverse_rms = lax.rsqrt(square_total / D + 1e-06)
    gain_here = lax.dynamic_slice_in_dim(
        norm_gain, lax.axis_index("tensor") * width_here, width_here
    )
    normed_part = (level * inverse_rms[:, None] * gain_here[None, :]).astype(jnp.bfloat16)
    normed = lax.all_gather(normed_part, "tensor", axis=1, tiled=True)
    columns = normed
    lifted = jnp.dot(
        columns,
        lax.all_gather(up_weight, "seq", axis=0, tiled=True),
        preferred_element_type=jnp.float32,
    )
    expanded = jax.nn.gelu(lifted, approximate=True).astype(jnp.bfloat16)
    return (residual_out, expanded)


def solution(mesh):
    in_specs = (
        P("seq", "tensor"),
        P("seq", "tensor"),
        P("seq", "tensor"),
        P("seq", "tensor"),
        P("tensor", None),
        P(),
        P("seq", "tensor"),
    )
    out_specs = (P("seq", "tensor"), P("seq", "tensor"))
    return jax.shard_map(body, mesh=mesh, in_specs=in_specs, out_specs=out_specs, check_vma=False)
```

profile of v0, /device:TPU:1, one launch (start us, length us, event | category | flops | bytes accessed | tf_op | source)
XLA Modules:
  0.0 418.1 jit_solution(12184925633184226929)
XLA Ops:
  7.2 0.0 all-gather.5.cloned.1.call-start
  7.2 1.9 copy.17
  9.1 0.0 all-gather.5.cloned.1.call-update
  9.1 0.0 all-gather.7.cloned.1.call-start
  9.2 0.7 all-gather.7.cloned.1.call-update
  9.9 0.0 reduce-scatter.4.cloned.1.call-start
  9.9 1.2 copy.16
  11.1 66.6 %all-gather.5.cloned.1.call-done = bf16[4096,384]{0,1:T(8,128)(2,1)} async-done(((bf16[512,384]{0,1:T(8,128)(2,1)}), bf16[4096,384]{0,1:T(8,128)(2,1)}) %all-gather.5.cloned.1.call-update) | async-done | bytes 3145744 | tf_op jit(solution)/shard_map/all_gather | solution.py:20
  77.7 5.5 %multiply_reduce_fusion = (f32[3,512]{1,0:T(4,128)S(1)}, f32[3,512,4096]{2,1,0:T(8,128)S(1)}) fusion(bf16[512,3,128]{0,2,1:T(8,128)(2,1)S(1)} %bitcast.37, bf16[4096,3,128]{0,2,1:T(8,128)(2,1)} %bitcast.36), kind=kOutput, calls=%fused_computation.1 | convolution fusion | flops 1623194112 | bytes 28710912 | tf_op jit(solution)/shard_map/thd,shd->hts/dot_general | solution.py:26
  83.1 0.0 copy-start
  83.2 5.0 %fusion = f32[3,512]{1,0:T(4,128)S(1)} fusion(f32[3,512,4096]{2,1,0:T(8,128)S(1)} %get-tuple-element.5, f32[3,512]{1,0:T(4,128)S(1)} %get-tuple-element.4), kind=kLoop, calls=%fused_computation.2 | loop fusion | flops 18872832 | bytes 25178112 | tf_op jit(solution)/shard_map/reduce_sum | solution.py:32
  88.1 3.7 copy-done
  91.9 48.7 %all-gather.7.cloned.1.call-done = bf16[4096,384]{1,0:T(8,128)(2,1)} async-done(((bf16[512,384]{1,0:T(8,128)(2,1)}), bf16[4096,384]{1,0:T(8,128)(2,1)}) %all-gather.7.cloned.1.call-update) | async-done | bytes 3145744 | tf_op jit(solution)/shard_map/all_gather | solution.py:21
  140.6 0.0 slice-start
  140.6 4.8 %copy.20 = bf16[4096,384]{0,1:T(8,128)(2,1)} copy(bf16[4096,384]{1,0:T(8,128)(2,1)} %all-gather.7.cloned.1.call-done) | data formatting | bytes 6291456 | tf_op jit(solution)/shard_map/all_gather | solution.py:21
  145.4 0.0 slice-start.1
  145.4 11.8 %fusion.22 = bf16[512,3,128]{0,2,1:T(8,128)(2,1)S(1)} fusion(bf16[4096,3,128]{0,2,1:T(8,128)(2,1)} %bitcast.35, f32[3,512,4096]{2,1,0:T(8,128)} %copy-done, f32[3,512]{1,0:T(4,128)S(1)} %get-tuple-element.4, f32[512,3]{0,1:T(4,128)S(1)} %bitcast_add_fusion.1, f32[512,3]{0,1:T(4,128)S(1)} %multiply_bitcast_fusion), kind=kOutput, calls=%fused_computation.19 | convolution fusion | flops 1630076928 | bytes 28723200 | tf_op jit(solution)/shard_map/hts,shd->htd/dot_general | solution.py:33
  157.2 0.0 slice-done
  157.2 0.0 slice-done.1
  157.2 5.4 %fusion.4 = bf16[6144,512]{0,1:T(8,128)(2,1)} fusion(bf16[512,384]{0,1:T(8,128)(2,1)S(1)} %bitcast.38, bf16[384,6144]{1,0:T(8,128)(2,1)S(1)} %bitcast.34), kind=kOutput, calls=%fused_computation.6 | convolution fusion | flops 2419064832 | bytes 11403264 | tf_op jit(solution)/shard_map/dot_general | solution.py:45
  162.7 8.7 %copy.23 = bf16[6144,512]{1,0:T(8,128)(2,1)} copy(bf16[6144,512]{0,1:T(8,128)(2,1)} %fusion.4) | data formatting | bytes 12582912
  171.4 0.0 copy-start.2
  171.4 0.0 reduce-scatter.4.cloned.1.call-update
  171.4 0.0 all-gather.11.cloned.1.call-start
  171.4 0.5 all-gather.11.cloned.1.call-update
  172.0 0.0 all-gather.9.cloned.1.call-start
  172.0 0.8 dynamic_slice.3
  172.8 63.7 %reduce-scatter.4.cloned.1.call-done = bf16[384,512]{1,0:T(8,128)(2,1)} async-done(((bf16[6144,512]{1,0:T(8,128)(2,1)}), bf16[384,512]{1,0:T(8,128)(2,1)}) %reduce-scatter.4.cloned.1.call-update) | async-done | bytes 393232
  236.5 1.2 copy.24
  237.7 0.0 copy-done.2
  237.7 0.2 fusion.25
  238.0 0.0 copy-start.1
  238.0 31.6 %psum.7 = f32[512]{0:T(512)S(1)} all-reduce(f32[512]{0:T(512)S(1)} %get-tuple-element.2), channel_id=1, replica_groups=mesh['seq'=8,'tensor'=16] {'tensor'}, use_global_device_ids=true, to_apply=%region_4.0 | all-reduce | flops 512 | bytes 4096 | tf_op jit(solution)/shard_map/psum | solution.py:55
  269.6 0.9 fusion.27
  270.5 0.0 all-gather.9.cloned.1.call-update
  270.5 86.9 %all-gather.11.cloned.1.call-done = bf16[6144,768]{1,0:T(8,128)(2,1)} async-done(((bf16[768,768]{1,0:T(8,128)(2,1)}), bf16[6144,768]{1,0:T(8,128)(2,1)}) %all-gather.11.cloned.1.call-update) | async-done | bytes 9437200 | tf_op jit(solution)/shard_map/all_gather | solution.py:65
  357.4 43.3 %all-gather.9.cloned.1.call-done = bf16[512,6144]{1,0:T(8,128)(2,1)} async-done(((bf16[512,384]{1,0:T(8,128)(2,1)}), bf16[512,6144]{1,0:T(8,128)(2,1)}) %all-gather.9.cloned.1.call-update) | async-done | bytes 6291472 | tf_op jit(solution)/shard_map/all_gather | solution.py:61
  400.7 10.8 %fusion.12 = bf16[512,768]{1,0:T(8,128)(2,1)} fusion(bf16[512,6144]{1,0:T(8,128)(2,1)} %all-gather.9.cloned.1.call-done, bf16[6144,768]{1,0:T(8,128)(2,1)} %all-gather.11.cloned.1.call-done), kind=kOutput, calls=%fused_computation.15 | convolution fusion | flops 4835377152 | bytes 16515072 | tf_op jit(solution)/shard_map/dot_general | solution.py:63
  411.5 0.0 copy-done.1
  (4 shorter events, 0.0 us)
Async XLA Ops:
  7.2 70.5 %all-gather.5.cloned.1.call-start = ((), (), s32[]{:S(2)}) async-start(), calls=%async_computation.1 | async-start | bytes 3538944 | tf_op jit(solution)/shard_map/all_gather | solution.py:20
  9.1 131.5 %all-gather.7.cloned.1.call-start = ((), (), s32[]{:S(2)}) async-start(), calls=%async_computation.2 | async-start | bytes 3538944 | tf_op jit(solution)/shard_map/all_gather | solution.py:21
  9.9 226.6 %reduce-scatter.4.cloned.1.call-start = ((), (), s32[]{:S(2)}) async-start(), calls=%async_computation.5 | async-start | bytes 6684672
  83.1 8.7 %copy-start = (f32[3,512,4096]{2,1,0:T(8,128)}, f32[3,512,4096]{2,1,0:T(8,128)S(1)}, u32[]{:S(2)}) copy-start(f32[3,512,4096]{2,1,0:T(8,128)S(1)} %get-tuple-element.5) | copy-start | bytes 75497472
  140.6 16.6 %slice-start = ((s8[4718592]{0:T(1024)(128)(4,1)}), s8[524288]{0:T(1024)(128)(4,1)S(1)}, s32[]{:S(2)}) async-start(s8[4718592]{0:T(1024)(128)(4,1)} %bitcast.33), calls=%async_computation.6 | async-start | bytes 1048576
  145.4 11.9 %slice-start.1 = ((s8[4718592]{0:T(1024)(128)(4,1)}), s8[4194304]{0:T(1024)(128)(4,1)S(1)}, s32[]{:S(2)}) async-start(s8[4718592]{0:T(1024)(128)(4,1)} %bitcast.33), calls=%async_computation.7 | async-start | bytes 8388608
  171.4 66.4 %copy-start.2 = (bf16[512,384]{1,0:T(8,128)(2,1)S(1)}, bf16[512,384]{1,0:T(8,128)(2,1)}, u32[]{:S(2)}) copy-start(bf16[512,384]{1,0:T(8,128)(2,1)} %param.10) | copy-start | bytes 1179652
  171.4 186.0 %all-gather.11.cloned.1.call-start = ((), (), s32[]{:S(2)}) async-start(), calls=%async_computation.4 | async-start | bytes 10616832 | tf_op jit(solution)/shard_map/all_gather | solution.py:65
  172.0 228.7 %all-gather.9.cloned.1.call-start = ((), (), s32[]{:S(2)}) async-start(), calls=%async_computation.3 | async-start | bytes 6684672 | tf_op jit(solution)/shard_map/all_gather | solution.py:61
  238.0 173.6 %copy-start.1 = (bf16[512,384]{1,0:T(8,128)(2,1)}, bf16[512,384]{1,0:T(8,128)(2,1)S(1)}, u32[]{:S(2)}) copy-start(bf16[512,384]{1,0:T(8,128)(2,1)S(1)} %get-tuple-element.3) | copy-start | bytes 1179652
Sparse Core Ops, SparseCore 0:
  10.8 66.8 all-gather.4
  80.0 60.5 all-gather.6
  171.5 64.9 reduce-scatter.3
  238.7 118.7 all-gather.10
  359.5 41.1 all-gather.8
where the time goes:
time: 419 us; the launch traced here: 418 us
  waiting for transfers between devices  310 us (74%)
  matrix products  33.5 us (8%)
  blocking collectives  31.6 us (8%)
  local copies, waits for them, and re-layouts  22.3 us (5%)
  between operations  13.9 us (3%)
  other arithmetic  6.13 us (1%)
    all_gather x1, waiting for transfers between devices, body(): lax.all_gather(up_weight, 'seq', axis=0, tiled=True)  86.9 us
    all_gather x1, waiting for transfers between devices, body(): key_piece = lax.all_gather(keys, 'seq', axis=0, tiled=True)  66.6 us
    unnamed x6, waiting for transfers between devices  65 us
    all_gather x1, waiting for transfers between devices, body(): value_piece = lax.all_gather(values, 'seq', axis=0, tiled=True)  48.7 us
    all_gather x1, waiting for transfers between devices, body(): normed = lax.all_gather(normed_part, 'tensor', axis=1, tiled=True)  43.3 us
    psum x1, blocking collectives, body(): square_total = lax.psum(partial_squares, 'tensor')  31.6 us
    unnamed x14, local copies, waits for them, and re-layouts  16.7 us
    dot_general x1, matrix products, body(): jnp.einsum('hts,shd->htd', weights.astype(jnp.bfloat16), value_heads, pre...  11.8 us
  transfers between devices with their start and end apart: 5, of which 5 were waited for; matrix products, arithmetic and copies ran while one was open for 4% of the time, Pallas kernels for 0%

commit v1 on v0

v1 whole, which is shorter than its diff:
```python
import math

import jax
import jax.numpy as jnp
from jax import lax
from jax.experimental import pallas as pl
from jax.experimental.pallas import tpu as pltpu
from jax.sharding import PartitionSpec as P

D = 6144
HD = 128
EXPONENT = math.log2(math.e) / math.sqrt(HD)
MESH = pl.DeviceIdType.MESH
BF16 = jnp.bfloat16
F32 = jnp.float32

ROWS = 512
HALF = 256
OWN = 384
WIDE = 768
SPLIT = 384


class Copies:
    def __init__(self, send, recv):
        self.send, self.recv, self.made = send, recv, {}

    def __call__(self, name, src, dst, device):
        index = len(self.made)
        self.made[name] = pltpu.make_async_remote_copy(
            src_ref=src,
            dst_ref=dst,
            send_sem=self.send.at[index],
            recv_sem=self.recv.at[index],
            device_id=device,
            device_id_type=MESH,
        )
        self.made[name].start()

    def arrive(self, *names):
        for name in names:
            self.made[name].wait_recv()

    def finish(self):
        for copy in self.made.values():
            copy.wait_send()


N_REMOTE = 96
N_LOCAL = 32


def kernel(
    q_ref, k_ref, v_ref, stream_ref, ow_ref, gain_ref, up_ref,
    residual_ref, expanded_ref,
    qb, kvb, o_out, st_out, o_in, st_in, o_own, st_own, att, owb, wb, stream_vm,
    p_far, p_plus, p_minus, p_here, r_far, r_plus, r_minus, y_out, y_in, xb, total, squares, result,
    send, recv, local_sem,
):
    s = lax.axis_index("seq")
    t = lax.axis_index("tensor")
    z, yh = s // 2, lax.rem(s, 2)
    yl, x, c = t // 8, lax.rem(t // 2, 4), lax.rem(t, 2)

    def ring(a, d):
        return lax.rem(a + d + 4, 4)

    def token_block(dz, dy):
        return ring(z, dz) * 2 + (yh if dy == 0 else 1 - yh)

    def chip(dy, dx):
        return (yl if dy == 0 else 1 - yl) * 4 + ring(x, dx)

    zp, zm = (token_block(1, 0), t), (token_block(-1, 0), t)
    yp = (token_block(0, 1), t)
    xp, xm = (s, chip(0, 1) * 2 + c), (s, chip(0, -1) * 2 + c)
    yq = (s, chip(1, 0) * 2 + c)
    cp = (s, chip(0, 0) * 2 + 1 - c)
    partners = (zp, zm, yp, xp, xm, yq, cp)

    barrier = pltpu.get_barrier_semaphore()
    for device in partners:
        pl.semaphore_signal(barrier, inc=1, device_id=device, device_id_type=MESH)

    locals_ = []

    def local(src, dst):
        copy = pltpu.make_async_copy(src, dst, local_sem.at[len(locals_)])
        copy.start()
        locals_.append(copy)
        return copy

    def head_columns(h):
        return pl.ds(h * HD, HD)

    kv_local = [
        [local(k_ref.at[:, head_columns(h)], kvb.at[h, 0, 0]), local(v_ref.at[:, head_columns(h)], kvb.at[h, 0, 1])]
        for h in range(3)
    ]
    q_local = [local(q_ref.at[:, head_columns(h)], qb.at[0, h]) for h in range(3)]
    w_local = local(up_ref, wb.at[s])
    mine = pl.ds(pl.multiple_of(c * OWN, 128), OWN)
    other = pl.ds(pl.multiple_of((1 - c) * OWN, 128), OWN)

    def feature_block(j, core):
        return pl.ds(pl.multiple_of((2 * j + core) * OWN, 128), OWN)

    ow_local = [local(ow_ref.at[:, feature_block(j, c)], owb.at[j, mine, :]) for j in range(8)]
    stream_local = local(stream_ref, stream_vm)

    pl.semaphore_wait(barrier, len(partners))
    go = Copies(send, recv)

    lower, upper = pl.ds(0, HALF), pl.ds(HALF, HALF)

    def near(h):
        go(f"n+{h}", kvb.at[h, 0], kvb.at[h, 1], zp)
        go(f"n-{h}", kvb.at[h, 0], kvb.at[h, 2], zm)

    def far(h):
        go.arrive(f"n+{h}")
        go(f"f+{h}", kvb.at[h, 1, :, lower], kvb.at[h, 3, :, lower], zp)
        go.arrive(f"n-{h}")
        go(f"f-{h}", kvb.at[h, 2, :, upper], kvb.at[h, 3, :, upper], zm)

    def attend(which, h):
        def tile(i, carry):
            rows = pl.ds(pl.multiple_of(i * HALF, HALF), HALF)
            scores = lax.dot_general(
                qb[which, h, rows, :],
                kvb[h, :, 0].reshape(4 * ROWS, HD),
                (((1,), (1,)), ((), ())),
                preferred_element_type=F32,
            )
            top = jnp.max(scores, axis=1, keepdims=True)
            weights = jnp.exp2((scores - top) * EXPONENT)
            bottom = jnp.sum(weights, axis=1, keepdims=True)
            out = jnp.dot(
                weights.astype(BF16), kvb[h, :, 1].reshape(4 * ROWS, HD), preferred_element_type=F32
            )
            out = out / bottom
            lane = lax.broadcasted_iota(jnp.int32, (HALF, HD), 1)
            both = jnp.where(lane == 0, top, bottom)
            if which == 1:
                o_out[h, rows, :] = out.astype(BF16)
                st_out[h, :, rows] = both.T[:8]
            else:
                o_own[h, rows, :] = out
                st_own[h, rows, :] = both
            return carry

        lax.fori_loop(0, 2, tile, 0)

    def give_back(h):
        go(f"o{h}", o_out.at[h], o_in.at[h], yp)
        go(f"s{h}", st_out.at[h], st_in.at[h], yp)

    for copy in kv_local[0]:
        copy.wait()
    near(0)
    for h in range(3):
        q_local[h].wait()
        go(f"q{h}", qb.at[0, h], qb.at[1, h], yp)
    for j in range(8):
        go(f"ow{j}", ow_ref.at[:, feature_block(j, 1 - c)], owb.at[j, mine, :], cp)
    for copy in kv_local[1] + kv_local[2]:
        copy.wait()
    w_local.wait()
    first, second = pl.ds(0, SPLIT), pl.ds(SPLIT, WIDE - SPLIT)
    far(0)
    near(1)
    go("wy1", wb.at[s, first], wb.at[s, first], yp)
    go("wy2", wb.at[s, second], wb.at[s, second], yp)
    go.arrive("f+0", "f-0", "q0")
    attend(1, 0)
    give_back(0)
    far(1)
    near(2)
    attend(0, 0)
    go.arrive("f+1", "f-1", "q1")
    attend(1, 1)
    give_back(1)
    far(2)
    attend(0, 1)
    go.arrive("f+2", "f-2", "q2")
    go("wz2+", wb.at[s, second], wb.at[s, second], zp)
    go("wz2-", wb.at[s, second], wb.at[s, second], zm)
    go("wz1+", wb.at[s, first], wb.at[s, first], zp)
    go("wz1-", wb.at[s, first], wb.at[s, first], zm)
    attend(1, 2)
    give_back(2)
    attend(0, 2)

    for h in range(3):
        go.arrive(f"o{h}", f"s{h}")
        theirs = jnp.concatenate([st_in[h]] * 16, axis=0).T
        top1, sum1 = st_own[h][:, 0:1], st_own[h][:, 1:2]
        top2, sum2 = theirs[:, 0:1], theirs[:, 1:2]
        top = jnp.maximum(top1, top2)
        w1 = sum1 * jnp.exp2((top1 - top) * EXPONENT)
        w2 = sum2 * jnp.exp2((top2 - top) * EXPONENT)
        scale = 1.0 / (w1 + w2)
        merged = (w1 * scale) * o_own[h] + (w2 * scale) * o_in[h].astype(F32)
        att[:, pl.ds(pl.multiple_of(c * OWN + h * HD, HD), HD)] = merged.astype(BF16)
    go("att", att.at[:, mine], att.at[:, mine], cp)
    for copy in ow_local:
        copy.wait()
    go.arrive(*[f"ow{j}" for j in range(8)])
    go.arrive("att")

    def project(dy, dx):
        return jnp.dot(att[...], owb[chip(dy, dx)], preferred_element_type=F32)

    for dy in (1, 0):
        p_far[dy] = project(dy, 2).astype(BF16)
        go(f"far+{dy}", p_far.at[dy, lower], r_far.at[dy, lower], xp)
        go(f"far-{dy}", p_far.at[dy, upper], r_far.at[dy, upper], xm)
        p_plus[dy] = project(dy, 1)
        p_minus[dy] = project(dy, -1)
        y_out[0, dy, upper, :] = p_plus[dy, upper, :].astype(BF16)
        y_out[1, dy, lower, :] = p_minus[dy, lower, :].astype(BF16)
        go(f"early+{dy}", y_out.at[0, dy, upper], r_plus.at[dy, upper], xp)
        go(f"early-{dy}", y_out.at[1, dy, lower], r_minus.at[dy, lower], xm)
    for dy in (1, 0):
        p_here[dy] = project(dy, 0)
    for dy in (1, 0):
        go.arrive(f"far+{dy}")
        y_out[0, dy, lower, :] = (p_plus[dy, lower, :] + r_far[dy, lower, :].astype(F32)).astype(BF16)
        go(f"late+{dy}", y_out.at[0, dy, lower], r_plus.at[dy, lower], xp)
        go.arrive(f"far-{dy}")
        y_out[1, dy, upper, :] = (p_minus[dy, upper, :] + r_far[dy, upper, :].astype(F32)).astype(BF16)
        go(f"late-{dy}", y_out.at[1, dy, upper], r_minus.at[dy, upper], xm)
    before, after, across = token_block(-1, 0), token_block(1, 0), token_block(2, 0)
    opposite = token_block(0, 1)
    go.arrive("wz2+")
    go("wq1", wb.at[before, second], wb.at[before, second], yp)
    go.arrive("wz2-")
    go("wf2", wb.at[after, second], wb.at[after, second], zm)
    go("wq2", wb.at[after, second], wb.at[after, second], yp)

    def near_sum(dy):
        go.arrive(f"early+{dy}", f"early-{dy}", f"late+{dy}", f"late-{dy}")
        return p_here[dy] + r_plus[dy].astype(F32) + r_minus[dy].astype(F32)

    y_in[0] = near_sum(1).astype(BF16)
    go("rows", y_in.at[0], y_in.at[1], yq)
    go.arrive("wz1+")
    go("wf1", wb.at[before, first], wb.at[before, first], zp)
    go.arrive("wz1-", "wy1")
    go("wp+", wb.at[opposite, first], wb.at[opposite, first], zp)
    go("wp-", wb.at[opposite, first], wb.at[opposite, first], zm)
    stream_local.wait()
    here = near_sum(0) + stream_vm[...].astype(F32)
    go.arrive("rows")
    own = chip(0, 0)
    xb[own, :, mine] = (here + y_in[1].astype(F32)).astype(BF16)
    residual_out = local(xb.at[own, :, mine], residual_ref)

    go("xc", xb.at[own, :, mine], xb.at[own, :, mine], cp)
    go("xy", xb.at[own, :, mine], xb.at[own, :, mine], yq)
    go("x+0", xb.at[own, :, mine], xb.at[own, :, mine], xp)
    go("x-0", xb.at[own, :, mine], xb.at[own, :, mine], xm)

    def pass_on(dy):
        left, right, far_chip = chip(dy, -1), chip(dy, 1), chip(dy, 2)
        go.arrive(f"x+{dy}")
        go(f"xf+{dy}", xb.at[left, lower, mine], xb.at[left, lower, mine], xp)
        go(f"xc+{dy}", xb.at[left, :, mine], xb.at[left, :, mine], cp)
        go.arrive(f"x-{dy}")
        go(f"xf-{dy}", xb.at[right, upper, mine], xb.at[right, upper, mine], xm)
        go(f"xc-{dy}", xb.at[right, :, mine], xb.at[right, :, mine], cp)

    def pass_far(dy):
        far_chip = chip(dy, 2)
        go.arrive(f"xf+{dy}", f"xf-{dy}")
        go(f"xcf{dy}", xb.at[far_chip, :, mine], xb.at[far_chip, :, mine], cp)

    def expand(j, start=False):
        gain = gain_ref[:, pl.ds(pl.multiple_of(j * WIDE, 128), WIDE)]
        level = xb[j].astype(F32)
        sums = jnp.sum(level * level, axis=1, keepdims=True)
        scaled = (level * gain).astype(BF16)
        product = jnp.dot(scaled, wb[j], preferred_element_type=F32)
        if start:
            squares[...] = jnp.broadcast_to(sums, (ROWS, 128))
            total[...] = product
        else:
            squares[...] += jnp.broadcast_to(sums, (ROWS, 128))
            total[...] += product

    far_opposite, before_opposite, after_opposite = token_block(2, 1), token_block(-1, 1), token_block(1, 1)
    q1, q2 = pl.ds(0, SPLIT // 2), pl.ds(SPLIT // 2, SPLIT // 2)
    pass_on(0)
    go.arrive("xy")
    other_chip = chip(1, 0)
    go("x+1", xb.at[other_chip, :, mine], xb.at[other_chip, :, mine], xp)
    go("x-1", xb.at[other_chip, :, mine], xb.at[other_chip, :, mine], xm)
    go("xcy", xb.at[other_chip, :, mine], xb.at[other_chip, :, mine], cp)
    go.arrive("wf2")
    go("wq3", wb.at[across, second], wb.at[across, second], yp)
    go.arrive("wp+")
    go("wpf+", wb.at[before_opposite, q1], wb.at[before_opposite, q1], zp)
    go.arrive("wp-")
    go("wpf-", wb.at[after_opposite, q2], wb.at[after_opposite, q2], zm)
    pass_far(0)
    pass_on(1)
    go.arrive("wy2", "wf1", "wpf+", "wpf-", "wq1", "wq2", "wq3")
    go.arrive("xc")
    expand(own, start=True)
    go.arrive("xc+0")
    expand(chip(0, -1))
    go.arrive("xc-0")
    expand(chip(0, 1))
    go.arrive("xcy")
    expand(chip(1, 0))
    go.arrive("xcf0")
    expand(chip(0, 2))
    go.arrive("xc+1")
    expand(chip(1, -1))
    go.arrive("xc-1")
    expand(chip(1, 1))
    pass_far(1)
    go.arrive("xcf1")
    expand(chip(1, 2))

    inverse = lax.rsqrt(squares[:, 0:1] * (1.0 / D) + 1e-6)
    result[...] = jax.nn.gelu(total[...] * inverse, approximate=True).astype(BF16)
    expanded_out = local(result, expanded_ref)
    go.finish()
    residual_out.wait()
    expanded_out.wait()


def body(queries, keys, values, stream, out_weight, norm_gain, up_weight):
    anywhere = pl.BlockSpec(memory_space=pl.ANY)
    vmem = pl.BlockSpec(memory_space=pltpu.VMEM)
    return pl.pallas_call(
        kernel,
        out_shape=(
            jax.ShapeDtypeStruct((ROWS, OWN), BF16),
            jax.ShapeDtypeStruct((ROWS, WIDE), BF16),
        ),
        in_specs=[anywhere, anywhere, anywhere, anywhere, anywhere, vmem, anywhere],
        out_specs=(anywhere, anywhere),
        scratch_shapes=[
            pltpu.VMEM((2, 3, ROWS, HD), BF16),
            pltpu.VMEM((3, 4, 2, ROWS, HD), BF16),
            pltpu.VMEM((3, ROWS, HD), BF16),
            pltpu.VMEM((3, 8, ROWS), F32),
            pltpu.VMEM((3, ROWS, HD), BF16),
            pltpu.VMEM((3, 8, ROWS), F32),
            pltpu.VMEM((3, ROWS, HD), F32),
            pltpu.VMEM((3, ROWS, HD), F32),
            pltpu.VMEM((ROWS, WIDE), BF16),
            pltpu.VMEM((8, WIDE, OWN), BF16),
            pltpu.VMEM((8, WIDE, WIDE), BF16),
            pltpu.VMEM((ROWS, OWN), BF16),
            pltpu.VMEM((2, ROWS, OWN), BF16),
            pltpu.VMEM((2, ROWS, OWN), F32),
            pltpu.VMEM((2, ROWS, OWN), F32),
            pltpu.VMEM((2, ROWS, OWN), F32),
            pltpu.VMEM((2, ROWS, OWN), BF16),
            pltpu.VMEM((2, ROWS, OWN), BF16),
            pltpu.VMEM((2, ROWS, OWN), BF16),
            pltpu.VMEM((2, 2, ROWS, OWN), BF16),
            pltpu.VMEM((2, ROWS, OWN), BF16),
            pltpu.VMEM((8, ROWS, WIDE), BF16),
            pltpu.VMEM((ROWS, WIDE), F32),
            pltpu.VMEM((ROWS, 128), F32),
            pltpu.VMEM((ROWS, WIDE), BF16),
            pltpu.SemaphoreType.DMA((N_REMOTE,)),
            pltpu.SemaphoreType.DMA((N_REMOTE,)),
            pltpu.SemaphoreType.DMA((N_LOCAL,)),
        ],
        compiler_params=pltpu.CompilerParams(
            collective_id=0, has_side_effects=True, vmem_limit_bytes=60 * 2**20
        ),
        cost_estimate=pl.CostEstimate(flops=10_500_000_000, bytes_accessed=12_000_000, transcendentals=6_300_000),
    )(queries, keys, values, stream, out_weight, norm_gain.reshape(1, D), up_weight)


def solution(mesh):
    in_specs = (
        P("seq", "tensor"),
        P("seq", "tensor"),
        P("seq", "tensor"),
        P("seq", "tensor"),
        P("tensor", None),
        P(),
        P("seq", "tensor"),
    )
    out_specs = (P("seq", "tensor"), P("seq", "tensor"))
    return jax.shard_map(body, mesh=mesh, in_specs=in_specs, out_specs=out_specs, check_vma=False)
```

time: 419 us -> 148 us (0.35)
  waiting for transfers between devices: 310 us -> 0 us
  Pallas kernels: 0 us -> 143 us
  matrix products: 33.5 us -> 0 us
  blocking collectives: 31.6 us -> 0 us
  local copies, waits for them, and re-layouts: 22.3 us -> 3.84 us
  between operations: 13.9 us -> 0.64 us
  other arithmetic: 6.13 us -> 0 us
    all_gather x4 -> x0, waiting for transfers between devices: 245 us -> none  [the longest x1 86.9 us: body(): lax.all_gather(up_weight, 'seq', axis=0, tiled=True)]
    pallas_call x0 -> x1, Pallas kernels: none -> 143 us  [body(): pl.pallas_call(kernel, out_shape=(jax.ShapeDtypeStruct((ROWS, OWN), BF16)...]
    unnamed x6 -> x0, waiting for transfers between devices: 65 us -> none
    dot_general x4 -> x0, matrix products: 33.5 us -> none  [the longest x1 11.8 us: body(): jnp.einsum('hts,shd->htd', weights.astype(jnp.bfloat16), value_heads, pre...]
    psum x1 -> x0, blocking collectives: 31.6 us -> none  [body(): square_total = lax.psum(partial_squares, 'tensor')]
    unnamed x14 -> x2, local copies, waits for them, and re-layouts: 16.7 us -> 3.84 us
    reduce_sum x2 -> x0, other arithmetic: 5.18 us -> none  [the longest x1 4.96 us: body(): new_sum = running_sum * decay_old + jnp.sum(weights, axis=2)]
    all_gather x1 -> x0, local copies, waits for them, and re-layouts: 4.76 us -> none  [body(): value_piece = lax.all_gather(values, 'seq', axis=0, tiled=True)]
  transfers between devices with their start and end apart: 5 -> 0, of which waited for: 5 -> 0; matrix products, arithmetic and copies ran while one was open for 4% -> 0% of each run, Pallas kernels for 0% -> 0%
where the time goes in v1:
time: 148 us
  Pallas kernels  143 us (97%)
  local copies, waits for them, and re-layouts  3.84 us (3%)
    pallas_call x1, Pallas kernels, body(): pl.pallas_call(kernel, out_shape=(jax.ShapeDtypeStruct((ROWS, OWN), BF16)...  143 us
    unnamed x2, local copies, waits for them, and re-layouts  3.84 us

profile of v1, /device:TPU:1, one launch (start us, length us, event | category | flops | bytes accessed | tf_op | source)
XLA Modules:
  0.0 147.6 jit_solution(5263752175555418498)
XLA Ops:
  0.6 143.1 %shard_map.86 = (bf16[512,384]{1,0:T(8,128)(2,1)}, bf16[512,768]{1,0:T(8,128)(2,1)}) custom-call(bf16[512,384]{1,0:T(8,128)(2,1)} %q_ref.1, bf16[512,384]{1,0:T(8,128)(2,1)} %k_ref.1, bf16[512,384]{1,0:T(8,128)(2,1)} %v_ref.1, bf16[512,384]{1,0:T(8,128)(2,1)} %stream_ref.1, bf16[384,6144]{1,0:T(8,128)(2,1)} %ow_ref.1, f32[1,6144]{1,0:T(1,128)} %bitcast.1, ...), custom_call_target="tpu_custom_call" | custom-call | flops 10499999744 | bytes 12000000 | tf_op jit(solution)/shard_map/pallas_call | solution.py:337
  143.8 1.8 %copy.11 = bf16[512,384]{1,0:T(8,128)(2,1)} copy(bf16[512,384]{1,0:T(8,128)(2,1)} %get-tuple-element.4) | data formatting | bytes 786432
  145.5 2.1 %copy.12 = bf16[512,768]{1,0:T(8,128)(2,1)} copy(bf16[512,768]{1,0:T(8,128)(2,1)} %get-tuple-element.5) | data formatting | bytes 1572864

commit v2 on v1

--- a/solution.py
+++ b/solution.py
@@ -18,7 +18,7 @@
 HALF = 256
 OWN = 384
 WIDE = 768
-SPLIT = 384
+SPLIT = 512
 
 
 class Copies:
@@ -158,41 +158,52 @@
     for copy in kv_local[0]:
         copy.wait()
     near(0)
+    for copy in kv_local[1]:
+        copy.wait()
+    near(1)
     for h in range(3):
         q_local[h].wait()
         go(f"q{h}", qb.at[0, h], qb.at[1, h], yp)
     for j in range(8):
         go(f"ow{j}", ow_ref.at[:, feature_block(j, 1 - c)], owb.at[j, mine, :], cp)
-    for copy in kv_local[1] + kv_local[2]:
+    for copy in kv_local[2]:
         copy.wait()
     w_local.wait()
     first, second = pl.ds(0, SPLIT), pl.ds(SPLIT, WIDE - SPLIT)
+    own_rows = token_block(0, 0)
+
+    def cross(i):
+        rows = pl.ds(i * 128, 128)
+        go(f"wy{i}", wb.at[own_rows, rows], wb.at[own_rows, rows], yp)
+
+    cross(0)
+    cross(1)
     far(0)
-    near(1)
-    go("wy1", wb.at[s, first], wb.at[s, first], yp)
-    go("wy2", wb.at[s, second], wb.at[s, second], yp)
+    near(2)
+    far(1)
     go.arrive("f+0", "f-0", "q0")
     attend(1, 0)
     give_back(0)
-    far(1)
-    near(2)
+    cross(2)
+    cross(3)
     attend(0, 0)
+    far(2)
+    go("wz2+", wb.at[own_rows, second], wb.at[own_rows, second], zp)
+    go("wz2-", wb.at[own_rows, second], wb.at[own_rows, second], zm)
+    go("wz1+", wb.at[own_rows, first], wb.at[own_rows, first], zp)
+    go("wz1-", wb.at[own_rows, first], wb.at[own_rows, first], zm)
     go.arrive("f+1", "f-1", "q1")
     attend(1, 1)
     give_back(1)
-    far(2)
     attend(0, 1)
     go.arrive("f+2", "f-2", "q2")
-    go("wz2+", wb.at[s, second], wb.at[s, second], zp)
-    go("wz2-", wb.at[s, second], wb.at[s, second], zm)
-    go("wz1+", wb.at[s, first], wb.at[s, first], zp)
-    go("wz1-", wb.at[s, first], wb.at[s, first], zm)
     attend(1, 2)
     give_back(2)
+    cross(4)
+    cross(5)
     attend(0, 2)
 
-    for h in range(3):
-        go.arrive(f"o{h}", f"s{h}")
+    def merge(h):
         theirs = jnp.concatenate([st_in[h]] * 16, axis=0).T
         top1, sum1 = st_own[h][:, 0:1], st_own[h][:, 1:2]
         top2, sum2 = theirs[:, 0:1], theirs[:, 1:2]
@@ -202,78 +213,111 @@
         scale = 1.0 / (w1 + w2)
         merged = (w1 * scale) * o_own[h] + (w2 * scale) * o_in[h].astype(F32)
         att[:, pl.ds(pl.multiple_of(c * OWN + h * HD, HD), HD)] = merged.astype(BF16)
-    go("att", att.at[:, mine], att.at[:, mine], cp)
+
+    for h in range(3):
+        go.arrive(f"o{h}", f"s{h}")
+        merge(h)
+        columns = pl.ds(pl.multiple_of(c * OWN + h * HD, HD), HD)
+        go(f"att{h}", att.at[:, columns], att.at[:, columns], cp)
     for copy in ow_local:
         copy.wait()
     go.arrive(*[f"ow{j}" for j in range(8)])
-    go.arrive("att")
+    before, after, across = token_block(-1, 0), token_block(1, 0), token_block(2, 0)
+    opposite = token_block(0, 1)
+    before_opposite, after_opposite = token_block(-1, 1), token_block(1, 1)
+    go.arrive("wz2+")
+    go("wq1", wb.at[before, second], wb.at[before, second], yp)
+    go.arrive("att0", "att1", "att2")
 
     def project(dy, dx):
         return jnp.dot(att[...], owb[chip(dy, dx)], preferred_element_type=F32)
 
-    for dy in (1, 0):
-        p_far[dy] = project(dy, 2).astype(BF16)
+    def send_far(dy):
         go(f"far+{dy}", p_far.at[dy, lower], r_far.at[dy, lower], xp)
         go(f"far-{dy}", p_far.at[dy, upper], r_far.at[dy, upper], xm)
-        p_plus[dy] = project(dy, 1)
-        p_minus[dy] = project(dy, -1)
-        y_out[0, dy, upper, :] = p_plus[dy, upper, :].astype(BF16)
-        y_out[1, dy, lower, :] = p_minus[dy, lower, :].astype(BF16)
+
+    def send_early(dy):
         go(f"early+{dy}", y_out.at[0, dy, upper], r_plus.at[dy, upper], xp)
         go(f"early-{dy}", y_out.at[1, dy, lower], r_minus.at[dy, lower], xm)
-    for dy in (1, 0):
-        p_here[dy] = project(dy, 0)
-    for dy in (1, 0):
+
+    def send_late(dy):
         go.arrive(f"far+{dy}")
         y_out[0, dy, lower, :] = (p_plus[dy, lower, :] + r_far[dy, lower, :].astype(F32)).astype(BF16)
         go(f"late+{dy}", y_out.at[0, dy, lower], r_plus.at[dy, lower], xp)
         go.arrive(f"far-{dy}")
         y_out[1, dy, upper, :] = (p_minus[dy, upper, :] + r_far[dy, upper, :].astype(F32)).astype(BF16)
         go(f"late-{dy}", y_out.at[1, dy, upper], r_minus.at[dy, upper], xm)
-    before, after, across = token_block(-1, 0), token_block(1, 0), token_block(2, 0)
-    opposite = token_block(0, 1)
-    go.arrive("wz2+")
-    go("wq1", wb.at[before, second], wb.at[before, second], yp)
-    go.arrive("wz2-")
-    go("wf2", wb.at[after, second], wb.at[after, second], zm)
-    go("wq2", wb.at[after, second], wb.at[after, second], yp)
+
+    def near_blocks(dy):
+        p_plus[dy] = project(dy, 1)
+        p_minus[dy] = project(dy, -1)
+        y_out[0, dy, upper, :] = p_plus[dy, upper, :].astype(BF16)
+        y_out[1, dy, lower, :] = p_minus[dy, lower, :].astype(BF16)
 
     def near_sum(dy):
         go.arrive(f"early+{dy}", f"early-{dy}", f"late+{dy}", f"late-{dy}")
         return p_here[dy] + r_plus[dy].astype(F32) + r_minus[dy].astype(F32)
 
+    p_far[1] = project(1, 2).astype(BF16)
+    send_far(1)
+    near_blocks(1)
+    send_early(1)
+    p_far[0] = project(0, 2).astype(BF16)
+    near_blocks(0)
+    send_late(1)
+    send_far(0)
+    send_early(0)
+    p_here[1] = project(1, 0)
+    p_here[0] = project(0, 0)
+    go.arrive("wz2-")
+    go("wf2", wb.at[after, second], wb.at[after, second], zm)
+    go.arrive("wy0", "wy1", "wy2", "wy3")
+    go("wp+", wb.at[opposite, first], wb.at[opposite, first], zp)
+    go("wp-", wb.at[opposite, first], wb.at[opposite, first], zm)
     y_in[0] = near_sum(1).astype(BF16)
     go("rows", y_in.at[0], y_in.at[1], yq)
+    half1, half2 = pl.ds(SPLIT, 128), pl.ds(SPLIT + 128, 128)
+    go("wq2a", wb.at[after, half1], wb.at[after, half1], yp)
+    send_late(0)
+    rows1, rows2 = pl.ds(0, WIDE // 2), pl.ds(WIDE // 2, SPLIT - WIDE // 2)
     go.arrive("wz1+")
-    go("wf1", wb.at[before, first], wb.at[before, first], zp)
-    go.arrive("wz1-", "wy1")
-    go("wp+", wb.at[opposite, first], wb.at[opposite, first], zp)
-    go("wp-", wb.at[opposite, first], wb.at[opposite, first], zm)
+    go("wf1", wb.at[before, rows1], wb.at[before, rows1], zp)
+    go.arrive("wz1-")
+    go("wf3", wb.at[after, rows2], wb.at[after, rows2], zm)
     stream_local.wait()
     here = near_sum(0) + stream_vm[...].astype(F32)
     go.arrive("rows")
     own = chip(0, 0)
     xb[own, :, mine] = (here + y_in[1].astype(F32)).astype(BF16)
-    residual_out = local(xb.at[own, :, mine], residual_ref)
-
-    go("xc", xb.at[own, :, mine], xb.at[own, :, mine], cp)
-    go("xy", xb.at[own, :, mine], xb.at[own, :, mine], yq)
-    go("x+0", xb.at[own, :, mine], xb.at[own, :, mine], xp)
-    go("x-0", xb.at[own, :, mine], xb.at[own, :, mine], xm)
+
+    def block(j, rows=slice(None)):
+        return xb.at[j, rows, mine]
+
+    def spread(dy):
+        j = chip(dy, 0)
+        go(f"x+{dy}a", block(j, lower), block(j, lower), xp)
+        go(f"x-{dy}a", block(j, upper), block(j, upper), xm)
+        go(f"x+{dy}b", block(j, upper), block(j, upper), xp)
+        go(f"x-{dy}b", block(j, lower), block(j, lower), xm)
 
     def pass_on(dy):
-        left, right, far_chip = chip(dy, -1), chip(dy, 1), chip(dy, 2)
-        go.arrive(f"x+{dy}")
-        go(f"xf+{dy}", xb.at[left, lower, mine], xb.at[left, lower, mine], xp)
-        go(f"xc+{dy}", xb.at[left, :, mine], xb.at[left, :, mine], cp)
-        go.arrive(f"x-{dy}")
-        go(f"xf-{dy}", xb.at[right, upper, mine], xb.at[right, upper, mine], xm)
-        go(f"xc-{dy}", xb.at[right, :, mine], xb.at[right, :, mine], cp)
+        left, right = chip(dy, -1), chip(dy, 1)
+        go.arrive(f"x+{dy}a")
+        go(f"xf+{dy}", block(left, lower), block(left, lower), xp)
+        go.arrive(f"x-{dy}a")
+        go(f"xf-{dy}", block(right, upper), block(right, upper), xm)
+
+    def pass_core(dy):
+        left, right = chip(dy, -1), chip(dy, 1)
+        go.arrive(f"x+{dy}b")
+        go(f"xc+{dy}", block(left), block(left), cp)
+        go.arrive(f"x-{dy}b")
+        go(f"xc-{dy}", block(right), block(right), cp)
 
     def pass_far(dy):
-        far_chip = chip(dy, 2)
+        j = chip(dy, 2)
         go.arrive(f"xf+{dy}", f"xf-{dy}")
-        go(f"xcf{dy}", xb.at[far_chip, :, mine], xb.at[far_chip, :, mine], cp)
+        go(f"xcf{dy}", block(j), block(j), cp)
 
     def expand(j, start=False):
         gain = gain_ref[:, pl.ds(pl.multiple_of(j * WIDE, 128), WIDE)]
@@ -288,23 +332,28 @@
             squares[...] += jnp.broadcast_to(sums, (ROWS, 128))
             total[...] += product
 
-    far_opposite, before_opposite, after_opposite = token_block(2, 1), token_block(-1, 1), token_block(1, 1)
-    q1, q2 = pl.ds(0, SPLIT // 2), pl.ds(SPLIT // 2, SPLIT // 2)
-    pass_on(0)
-    go.arrive("xy")
-    other_chip = chip(1, 0)
-    go("x+1", xb.at[other_chip, :, mine], xb.at[other_chip, :, mine], xp)
-    go("x-1", xb.at[other_chip, :, mine], xb.at[other_chip, :, mine], xm)
-    go("xcy", xb.at[other_chip, :, mine], xb.at[other_chip, :, mine], cp)
+    spread(0)
+    go("xy", block(own), block(own), yq)
+    go("xc", block(own), block(own), cp)
+    residual_out = local(block(own), residual_ref)
+    go("wq2b", wb.at[after, half2], wb.at[after, half2], yp)
     go.arrive("wf2")
     go("wq3", wb.at[across, second], wb.at[across, second], yp)
+    pass_on(0)
+    pass_core(0)
+    go.arrive("xy")
+    spread(1)
+    other_chip = chip(1, 0)
+    go("xcy", block(other_chip), block(other_chip), cp)
+    q1, q2 = pl.ds(0, SPLIT // 2), pl.ds(SPLIT // 2, SPLIT // 2)
     go.arrive("wp+")
     go("wpf+", wb.at[before_opposite, q1], wb.at[before_opposite, q1], zp)
     go.arrive("wp-")
     go("wpf-", wb.at[after_opposite, q2], wb.at[after_opposite, q2], zm)
     pass_far(0)
     pass_on(1)
-    go.arrive("wy2", "wf1", "wpf+", "wpf-", "wq1", "wq2", "wq3")
+    pass_core(1)
+    go.arrive("wy4", "wy5", "wf1", "wf3", "wq1", "wq2a", "wq2b", "wpf+", "wpf-", "wq3")
     go.arrive("xc")
     expand(own, start=True)
     go.arrive("xc+0")
@@ -323,12 +372,15 @@
     go.arrive("xcf1")
     expand(chip(1, 2))
 
-    inverse = lax.rsqrt(squares[:, 0:1] * (1.0 / D) + 1e-6)
-    result[...] = jax.nn.gelu(total[...] * inverse, approximate=True).astype(BF16)
-    expanded_out = local(result, expanded_ref)
+    outs = []
+    for rows in (lower, upper):
+        inverse = lax.rsqrt(squares[rows, 0:1] * (1.0 / D) + 1e-6)
+        result[rows] = jax.nn.gelu(total[rows] * inverse, approximate=True).astype(BF16)
+        outs.append(local(result.at[rows], expanded_ref.at[rows]))
     go.finish()
     residual_out.wait()
-    expanded_out.wait()
+    for copy in outs:
+        copy.wait()
 
 
 def body(queries, keys, values, stream, out_weight, norm_gain, up_weight):

time: 148 us -> 119 us (0.80)
  Pallas kernels: 143 us -> 114 us
    pallas_call x1, Pallas kernels: 143 us -> 114 us  [body(): pl.pallas_call(kernel, out_shape=(jax.ShapeDtypeStruct((ROWS, OWN), BF16)...]
where the time goes in v2:
time: 119 us; the launch traced here: 118 us
  Pallas kernels  114 us (96%)
  local copies, waits for them, and re-layouts  3.84 us (3%)
    pallas_call x1, Pallas kernels, body(): pl.pallas_call(kernel, out_shape=(jax.ShapeDtypeStruct((ROWS, OWN), BF16)...  114 us
    unnamed x2, local copies, waits for them, and re-layouts  3.84 us

profile of v2, /device:TPU:1, one launch (start us, length us, event | category | flops | bytes accessed | tf_op | source)
XLA Modules:
  0.0 118.4 jit_solution(8626071193741844313)
XLA Ops:
  0.6 113.9 %shard_map.86 = (bf16[512,384]{1,0:T(8,128)(2,1)}, bf16[512,768]{1,0:T(8,128)(2,1)}) custom-call(bf16[512,384]{1,0:T(8,128)(2,1)} %q_ref.1, bf16[512,384]{1,0:T(8,128)(2,1)} %k_ref.1, bf16[512,384]{1,0:T(8,128)(2,1)} %v_ref.1, bf16[512,384]{1,0:T(8,128)(2,1)} %stream_ref.1, bf16[384,6144]{1,0:T(8,128)(2,1)} %ow_ref.1, f32[1,6144]{1,0:T(1,128)} %bitcast.1, ...), custom_call_target="tpu_custom_call" | custom-call | flops 10499999744 | bytes 12000000 | tf_op jit(solution)/shard_map/pallas_call | solution.py:389
  114.5 1.8 %copy.11 = bf16[512,384]{1,0:T(8,128)(2,1)} copy(bf16[512,384]{1,0:T(8,128)(2,1)} %get-tuple-element.4) | data formatting | bytes 786432
  116.3 2.1 %copy.12 = bf16[512,768]{1,0:T(8,128)(2,1)} copy(bf16[512,768]{1,0:T(8,128)(2,1)} %get-tuple-element.5) | data formatting | bytes 1572864

commit v3 on v2

v3 whole, which is shorter than its diff:
```python
import math

import jax
import jax.numpy as jnp
from jax import lax
from jax.experimental import pallas as pl
from jax.experimental.pallas import tpu as pltpu
from jax.sharding import PartitionSpec as P

D = 6144
HD = 128
EXPONENT = math.log2(math.e) / math.sqrt(HD)
MESH = pl.DeviceIdType.MESH
BF16 = jnp.bfloat16
F32 = jnp.float32

ROWS = 512
HALF = 256
OWN = 384
WIDE = 768
SPLIT = 512


class Copies:
    def __init__(self, send, recv):
        self.send, self.recv = send, recv
        self.made, self.slots, self.groups = {}, {}, {}
        self.free, self.used = [], 0

    def __call__(self, name, src, dst, device, group=None):
        if not self.free:
            self.free.append(self.used)
            self.used += 1
        self.slots[name] = slot = self.free.pop()
        index = self.groups.setdefault(group or name, len(self.groups))
        self.made[name] = copy = pltpu.make_async_remote_copy(
            src_ref=src,
            dst_ref=dst,
            send_sem=self.send.at[slot],
            recv_sem=self.recv.at[index],
            device_id=device,
            device_id_type=MESH,
        )
        copy.start()

    def arrive(self, *names):
        for name in names:
            self.made[name].wait_recv()

    def arrive_all(self, group, ref, device):
        pltpu.make_async_remote_copy(
            src_ref=ref,
            dst_ref=ref,
            send_sem=self.send.at[0],
            recv_sem=self.recv.at[self.groups[group]],
            device_id=device,
            device_id_type=MESH,
        ).wait_recv()

    def drain(self, *names):
        for name in names or tuple(self.slots):
            self.made[name].wait_send()
            self.free.append(self.slots.pop(name))


N_SEND = 47
N_RECV = 66
N_LOCAL = 8


def kernel(
    q_ref, k_ref, v_ref, stream_ref, ow_ref, gain_ref, up_ref,
    residual_ref, expanded_ref,
    qb, kvb, o_out, st_out, o_in, st_in, o_part, st_part, att, owb, wb, stream_vm,
    p_far, p_out, p_plus, p_minus, p_here, r_far, r_plus, r_minus, y_out, y_in, xb, xg, total, squares,
    send, recv, local_sem,
):
    s = lax.axis_index("seq")
    t = lax.axis_index("tensor")
    z, yh = s // 2, lax.rem(s, 2)
    yl, x, c = t // 8, lax.rem(t // 2, 4), lax.rem(t, 2)

    def ring(a, d):
        return lax.rem(a + d + 4, 4)

    def token_block(dz, dy):
        return ring(z, dz) * 2 + (yh if dy == 0 else 1 - yh)

    def chip(dy, dx):
        return (yl if dy == 0 else 1 - yl) * 4 + ring(x, dx)

    zp, zm = (token_block(1, 0), t), (token_block(-1, 0), t)
    yp = (token_block(0, 1), t)
    xp, xm = (s, chip(0, 1) * 2 + c), (s, chip(0, -1) * 2 + c)
    yq = (s, chip(1, 0) * 2 + c)
    cp = (s, chip(0, 0) * 2 + 1 - c)
    partners = (zp, zm, yp, xp, xm, yq, cp)

    barrier = pltpu.get_barrier_semaphore()
    for device in partners:
        pl.semaphore_signal(barrier, inc=1, device_id=device, device_id_type=MESH)

    def local(index, *pairs):
        for src, dst in pairs:
            pltpu.make_async_copy(src, dst, local_sem.at[index]).start()

    def landed(index, ref):
        pltpu.make_async_copy(ref, ref, local_sem.at[index]).wait()

    def head_columns(h):
        return pl.ds(h * HD, HD)

    for h in range(3):
        local(
            h,
            (k_ref.at[:, head_columns(h)], kvb.at[h, 0, 0]),
            (v_ref.at[:, head_columns(h)], kvb.at[h, 0, 1]),
        )
    local(3, *[(q_ref.at[:, head_columns(h)], qb.at[0, h]) for h in range(3)])
    local(4, (up_ref, wb.at[s]))
    mine = pl.ds(pl.multiple_of(c * OWN, 128), OWN)

    def feature_block(j, core):
        return pl.ds(pl.multiple_of((2 * j + core) * OWN, 128), OWN)

    local(5, *[(ow_ref.at[:, :, feature_block(j, c)], owb.at[j, :, c]) for j in range(8)])
    local(6, (stream_ref, stream_vm))

    def greeted():
        pl.semaphore_wait(barrier, len(partners))

    greeted()
    go = Copies(send, recv)

    lower, upper = pl.ds(0, HALF), pl.ds(HALF, HALF)

    def near(h):
        go(f"n+{h}", kvb.at[h, 0], kvb.at[h, 1], zp)
        go(f"n-{h}", kvb.at[h, 0], kvb.at[h, 2], zm)

    def far(h):
        go.arrive(f"n+{h}")
        go(f"f+{h}", kvb.at[h, 1, :, lower], kvb.at[h, 3, :, lower], zp, f"f{h}")
        go.arrive(f"n-{h}")
        go(f"f-{h}", kvb.at[h, 2, :, upper], kvb.at[h, 3, :, upper], zm, f"f{h}")

    def scores_of(which, h, rows, slots):
        keys = kvb[h, slots, 0].reshape(-1, HD)
        return lax.dot_general(
            qb[which, h, rows, :], keys, (((1,), (1,)), ((), ())), preferred_element_type=F32
        )

    lane = lax.broadcasted_iota(jnp.int32, (HALF, HD), 1)

    def attend_near(which, h):
        def tile(i, carry):
            rows = pl.ds(pl.multiple_of(i * HALF, HALF), HALF)
            slots = slice(0, 3)
            scores = scores_of(which, h, rows, slots)
            top = jnp.max(scores, axis=1, keepdims=True)
            weights = jnp.exp2((scores - top) * EXPONENT)
            bottom = jnp.sum(weights, axis=1, keepdims=True)
            o_part[which, h, rows, :] = jnp.dot(
                weights.astype(BF16), kvb[h, slots, 1].reshape(-1, HD), preferred_element_type=F32
            )
            st_part[which, h, rows, :] = jnp.where(lane == 0, top, bottom)
            return carry

        lax.fori_loop(0, 2, tile, 0)

    def attend_far(which, h, halves=None):
        def tile(i, carry):
            rows = pl.ds(i * HALF if isinstance(i, int) else pl.multiple_of(i * HALF, HALF), HALF)
            slots = slice(3, 4)
            scores = scores_of(which, h, rows, slots)
            stats = st_part[which, h, rows, :]
            top_near, bottom_near = stats[:, 0:1], stats[:, 1:2]
            top = jnp.maximum(top_near, jnp.max(scores, axis=1, keepdims=True))
            weights = jnp.exp2((scores - top) * EXPONENT)
            decay = jnp.exp2((top_near - top) * EXPONENT)
            bottom = bottom_near * decay + jnp.sum(weights, axis=1, keepdims=True)
            out = jnp.dot(weights.astype(BF16), kvb[h, slots, 1].reshape(-1, HD), preferred_element_type=F32)
            out = (o_part[which, h, rows, :] * decay + out) / bottom
            both = jnp.where(lane == 0, top, bottom)
            if which == 1:
                o_out[h, rows, :] = out.astype(BF16)
                st_out[h, :, rows] = both.T[:8]
            else:
                o_part[0, h, rows, :] = out
                st_part[0, h, rows, :] = both
            return carry

        if halves is None:
            lax.fori_loop(0, 2, tile, 0)
        else:
            tile(halves, 0)

    def give_back(h, part="", rows=slice(None)):
        go(f"s{h}{part}", st_out.at[h, :, rows], st_in.at[h, :, rows], yp)
        go(f"o{h}{part}", o_out.at[h, rows], o_in.at[h, rows], yp)

    landed(0, kvb.at[0, 0])
    near(0)
    landed(1, kvb.at[1, 0])
    near(1)
    landed(3, qb.at[0])
    for h in range(3):
        go(f"q{h}", qb.at[0, h], qb.at[1, h], yp)
    for j in range(8):
        go(f"ow{j}", ow_ref.at[:, :, feature_block(j, 1 - c)], owb.at[j, :, c], cp, "ow")
    landed(2, kvb.at[2, 0])
    landed(4, wb.at[s])
    first, second = pl.ds(0, SPLIT), pl.ds(SPLIT, WIDE - SPLIT)
    own_rows = token_block(0, 0)

    def cross(i, n=2):
        rows = pl.ds(i * 64, n * 64)
        go(f"wy{i}", wb.at[own_rows, rows], wb.at[own_rows, rows], yp, "wy1" if i < SPLIT // 64 else "wy2")

    cross(0)
    cross(2)
    far(0)
    near(2)
    go.arrive("q0")
    attend_near(1, 0)
    attend_near(0, 0)
    far(1)
    go.arrive("q1")
    attend_near(1, 1)
    attend_near(0, 1)
    go.arrive_all("f0", kvb.at[0, 3], zp)
    attend_far(1, 0)
    give_back(0)
    cross(4)
    attend_far(0, 0)
    far(2)
    go("wz2+", wb.at[own_rows, second], wb.at[own_rows, second], zp)
    go("wz2-", wb.at[own_rows, second], wb.at[own_rows, second], zm)
    go("wz1+", wb.at[own_rows, first], wb.at[own_rows, first], zp)
    go("wz1-", wb.at[own_rows, first], wb.at[own_rows, first], zm)
    go.arrive("q2")
    attend_near(1, 2)
    attend_near(0, 2)
    go.arrive_all("f1", kvb.at[1, 3], zp)
    attend_far(1, 1)
    give_back(1)
    attend_far(0, 1)
    go.arrive_all("f2", kvb.at[2, 3], zp)
    attend_far(1, 2, 0)
    give_back(2, "a", lower)
    attend_far(1, 2, 1)
    give_back(2, "b", upper)
    cross(6)
    cross(8)
    cross(10)
    attend_far(0, 2)

    def merge(h, rows):
        theirs = jnp.concatenate([st_in[h, :, rows]] * 16, axis=0).T
        ours = st_part[0, h, rows, :]
        top1, sum1 = ours[:, 0:1], ours[:, 1:2]
        top2, sum2 = theirs[:, 0:1], theirs[:, 1:2]
        top = jnp.maximum(top1, top2)
        w1 = sum1 * jnp.exp2((top1 - top) * EXPONENT)
        w2 = sum2 * jnp.exp2((top2 - top) * EXPONENT)
        scale = 1.0 / (w1 + w2)
        merged = (w1 * scale) * o_part[0, h, rows, :] + (w2 * scale) * o_in[h, rows, :].astype(F32)
        att[h, rows, own_half] = merged.astype(BF16)

    own_half = pl.ds(pl.multiple_of(c * HD, HD), HD)
    whole = pl.ds(0, ROWS)
    for h in range(2):
        go.arrive(f"s{h}", f"o{h}")
        merge(h, whole)
        go(f"att{h}", att.at[h, :, own_half], att.at[h, :, own_half], cp, "att")
    go.drain(*[f"{kind}{h}" for kind in ("n+", "n-", "f+", "f-", "q") for h in range(3)], *[f"ow{j}" for j in range(8)])
    landed(5, owb.at[:, :, c])
    go.arrive_all("ow", owb.at[:, :, 1 - c], cp)
    go.arrive_all("att", att.at[0:2, :, own_half], cp)

    def project_two(dy, dx):
        return jnp.dot(
            jnp.concatenate([att[0], att[1]], axis=1),
            owb[chip(dy, dx), 0:2].reshape(4 * HD, OWN),
            preferred_element_type=F32,
        )

    def project_last(dy, dx, rows):
        return jnp.dot(
            att[2, rows, :], owb[chip(dy, dx), 2].reshape(2 * HD, OWN), preferred_element_type=F32
        )

    p_far[1] = project_two(1, 2)
    p_plus[1] = project_two(1, 1)
    p_minus[1] = project_two(1, -1)
    for part, rows in (("a", lower), ("b", upper)):
        go.arrive(f"s2{part}", f"o2{part}")
        merge(2, rows)
        go(f"att2{part}", att.at[2, rows, own_half], att.at[2, rows, own_half], cp)
    p_far[0] = project_two(0, 2)
    before, after, across = token_block(-1, 0), token_block(1, 0), token_block(2, 0)
    opposite = token_block(0, 1)
    before_opposite, after_opposite, across_opposite = token_block(-1, 1), token_block(1, 1), token_block(2, 1)

    def send_far(dy, rows):
        p_out[dy, rows, :] = (p_far[dy, rows, :] + project_last(dy, 2, rows)).astype(BF16)
        if rows is lower:
            go(f"far+{dy}", p_out.at[dy, rows], r_far.at[dy, rows], xp)
        else:
            go(f"far-{dy}", p_out.at[dy, rows], r_far.at[dy, rows], xm)

    def near_blocks(dy):
        p_plus[dy] += project_last(dy, 1, whole)
        y_out[0, dy, upper, :] = p_plus[dy, upper, :].astype(BF16)
        p_minus[dy] += project_last(dy, -1, whole)
        y_out[1, dy, lower, :] = p_minus[dy, lower, :].astype(BF16)

    def send_early(dy):
        go(f"early+{dy}", y_out.at[0, dy, upper], r_plus.at[dy, upper], xp, f"plus{dy}")
        go(f"early-{dy}", y_out.at[1, dy, lower], r_minus.at[dy, lower], xm, f"minus{dy}")

    def send_late(dy):
        go.arrive(f"far+{dy}")
        y_out[0, dy, lower, :] = (p_plus[dy, lower, :] + r_far[dy, lower, :].astype(F32)).astype(BF16)
        go(f"late+{dy}", y_out.at[0, dy, lower], r_plus.at[dy, lower], xp, f"plus{dy}")
        go.arrive(f"far-{dy}")
        y_out[1, dy, upper, :] = (p_minus[dy, upper, :] + r_far[dy, upper, :].astype(F32)).astype(BF16)
        go(f"late-{dy}", y_out.at[1, dy, upper], r_minus.at[dy, upper], xm, f"minus{dy}")

    def near_sum(dy):
        go.arrive_all(f"plus{dy}", r_plus.at[dy], xp)
        go.arrive_all(f"minus{dy}", r_minus.at[dy], xm)
        return p_here[dy] + r_plus[dy].astype(F32) + r_minus[dy].astype(F32)

    go.arrive("att2a")
    send_far(1, lower)
    go.arrive("att2b")
    send_far(1, upper)
    near_blocks(1)
    send_early(1)
    go.arrive("wz2+")
    go("wq1", wb.at[before, second], wb.at[before, second], yp)
    go.arrive("wz2-")
    go("wf2", wb.at[after, second], wb.at[after, second], zm)
    p_plus[0] = project_two(0, 1)
    p_minus[0] = project_two(0, -1)
    near_blocks(0)
    send_late(1)
    send_far(0, lower)
    send_far(0, upper)
    send_early(0)
    for dy in (1, 0):
        p_here[dy] = project_two(dy, 0) + project_last(dy, 0, whole)
    go.arrive_all("wy1", wb.at[opposite, first], yp)
    go("wp+", wb.at[opposite, first], wb.at[opposite, first], zp)
    go("wp-", wb.at[opposite, first], wb.at[opposite, first], zm)
    y_in[0] = near_sum(1).astype(BF16)
    go("rows", y_in.at[0], y_in.at[1], yq)
    half1, half2 = pl.ds(SPLIT, 128), pl.ds(SPLIT + 128, 128)
    go("wq2a", wb.at[after, half1], wb.at[after, half1], yp, "wq2")
    send_late(0)
    rows1, rows2 = pl.ds(0, WIDE // 2), pl.ds(WIDE // 2, SPLIT - WIDE // 2)
    go.arrive("wz1+")
    go("wf1", wb.at[before, rows1], wb.at[before, rows1], zp, "wf")
    go.arrive("wz1-")
    go("wf3", wb.at[after, rows2], wb.at[after, rows2], zm, "wf")
    landed(6, stream_vm)
    here = near_sum(0) + stream_vm[...].astype(F32)
    go.arrive("rows")
    own = chip(0, 0)
    residual = (here + y_in[1].astype(F32)).astype(BF16)
    xb[own, :, mine] = residual
    residual_ref[...] = residual

    def block(j, rows=slice(None)):
        return xb.at[j, rows, mine]

    def spread(dy):
        j = chip(dy, 0)
        go(f"x+{dy}a", block(j, lower), block(j, lower), xp)
        go(f"x-{dy}a", block(j, upper), block(j, upper), xm)
        go(f"x+{dy}b", block(j, upper), block(j, upper), xp)
        go(f"x-{dy}b", block(j, lower), block(j, lower), xm)

    def pass_on(dy):
        left, right = chip(dy, -1), chip(dy, 1)
        go.arrive(f"x+{dy}a")
        go(f"xf+{dy}", block(left, lower), block(left, lower), xp, f"xf{dy}")
        go.arrive(f"x-{dy}a")
        go(f"xf-{dy}", block(right, upper), block(right, upper), xm, f"xf{dy}")

    def pass_core(dy):
        left, right = chip(dy, -1), chip(dy, 1)
        go.arrive(f"x+{dy}b")
        go(f"xc+{dy}", block(left), block(left), cp)
        go.arrive(f"x-{dy}b")
        go(f"xc-{dy}", block(right), block(right), cp)

    def pass_far(dy):
        j = chip(dy, 2)
        go.arrive_all(f"xf{dy}", block(j), xp)
        go(f"xcf{dy}", block(j), block(j), cp)

    def prepare(j, start=False):
        gain = gain_ref[:, pl.ds(pl.multiple_of(j * WIDE, 128), WIDE)]
        level = xb[j].astype(F32)
        xg[j] = (level * gain).astype(BF16)
        level = level * level
        sums = level[:, 0:128]
        for k in range(1, WIDE // 128):
            sums = sums + level[:, k * 128 : (k + 1) * 128]
        squares[...] = sums if start else squares[...] + sums

    def expand(j, start=False):
        product = jnp.dot(xg[j], wb[j], preferred_element_type=F32)
        total[...] = product if start else total[...] + product

    go.drain(*[f"{kind}{sign}{dy}" for kind in ("far", "early", "late") for sign in "+-" for dy in (0, 1)])
    go.drain(*"s0 o0 s1 o1 s2a o2a s2b o2b att0 att1 att2a att2b wy0 wy2 wy4 wy6 wy8 wy10".split())
    go.drain("wz2+", "wz2-", "wz1+", "wz1-")
    spread(0)
    go("xy", block(own), block(own), yq)
    go("xc", block(own), block(own), cp)
    go("wq2b", wb.at[after, half2], wb.at[after, half2], yp, "wq2")
    go.arrive("wf2")
    go("wq3", wb.at[across, second], wb.at[across, second], yp)
    go.arrive("xc")
    prepare(own, start=True)
    pass_on(0)
    pass_core(0)
    go.arrive("xy")
    spread(1)
    other_chip = chip(1, 0)
    go("xcy", block(other_chip), block(other_chip), cp)
    q1, q2 = pl.ds(0, SPLIT // 2), pl.ds(SPLIT // 2, SPLIT // 2)
    go.arrive("wp+")
    go("wpf+", wb.at[before_opposite, q1], wb.at[before_opposite, q1], zp, "wpf")
    go.arrive("wp-")
    go("wpf-", wb.at[after_opposite, q2], wb.at[after_opposite, q2], zm, "wpf")
    go.arrive("xc+0")
    prepare(chip(0, -1))
    go.arrive("xc-0")
    prepare(chip(0, 1))
    pass_far(0)
    go.arrive("xcy")
    prepare(other_chip)
    pass_on(1)
    go.arrive("xcf0")
    prepare(chip(0, 2))
    go.arrive_all("wf", wb.at[across, first], zp)
    same = lax.rem(x + yh, 2)
    rest = 1 - same
    expand(chip(0, same), start=True)
    expand(chip(0, same + 2))
    go.arrive_all("wy2", wb.at[opposite, second], yp)
    go.arrive("wq1", "wq3")
    go.arrive_all("wq2", wb.at[after_opposite, second], yp)
    go.arrive_all("wpf", wb.at[across_opposite, first], zp)
    expand(chip(0, rest))
    pass_core(1)
    expand(chip(0, rest + 2))
    go.arrive("xc+1")
    prepare(chip(1, -1))
    go.arrive("xc-1")
    prepare(chip(1, 1))
    expand(other_chip)
    expand(chip(1, 1))
    pass_far(1)
    expand(chip(1, -1))
    go.arrive("xcf1")
    prepare(chip(1, 2))
    expand(chip(1, 2))

    for rows in (lower, upper):
        inverse = lax.rsqrt(jnp.sum(squares[rows], axis=1, keepdims=True) * (1.0 / D) + 1e-6)
        expanded_ref[rows] = jax.nn.gelu(total[rows] * inverse, approximate=True).astype(BF16)
    go.drain()
    assert go.used <= N_SEND and len(go.groups) <= N_RECV, (go.used, len(go.groups))


def body(queries, keys, values, stream, out_weight, norm_gain, up_weight):
    anywhere = pl.BlockSpec(memory_space=pl.ANY)
    vmem = pl.BlockSpec(memory_space=pltpu.VMEM)
    return pl.pallas_call(
        kernel,
        out_shape=(
            pltpu.VMEM((ROWS, OWN), BF16),
            pltpu.VMEM((ROWS, WIDE), BF16),
        ),
        in_specs=[anywhere, anywhere, anywhere, anywhere, anywhere, vmem, anywhere],
        out_specs=(vmem, vmem),
        scratch_shapes=[
            pltpu.VMEM((2, 3, ROWS, HD), BF16),
            pltpu.VMEM((3, 4, 2, ROWS, HD), BF16),
            pltpu.VMEM((3, ROWS, HD), BF16),
            pltpu.VMEM((3, 8, ROWS), F32),
            pltpu.VMEM((3, ROWS, HD), BF16),
            pltpu.VMEM((3, 8, ROWS), F32),
            pltpu.VMEM((2, 3, ROWS, HD), F32),
            pltpu.VMEM((2, 3, ROWS, HD), F32),
            pltpu.VMEM((3, ROWS, 2 * HD), BF16),
            pltpu.VMEM((8, 3, 2, HD, OWN), BF16),
            pltpu.VMEM((8, WIDE, WIDE), BF16),
            pltpu.VMEM((ROWS, OWN), BF16),
            pltpu.VMEM((2, ROWS, OWN), F32),
            pltpu.VMEM((2, ROWS, OWN), BF16),
            pltpu.VMEM((2, ROWS, OWN), F32),
            pltpu.VMEM((2, ROWS, OWN), F32),
            pltpu.VMEM((2, ROWS, OWN), F32),
            pltpu.VMEM((2, ROWS, OWN), BF16),
            pltpu.VMEM((2, ROWS, OWN), BF16),
            pltpu.VMEM((2, ROWS, OWN), BF16),
            pltpu.VMEM((2, 2, ROWS, OWN), BF16),
            pltpu.VMEM((2, ROWS, OWN), BF16),
            pltpu.VMEM((8, ROWS, WIDE), BF16),
            pltpu.VMEM((8, ROWS, WIDE), BF16),
            pltpu.VMEM((ROWS, WIDE), F32),
            pltpu.VMEM((ROWS, 128), F32),
            pltpu.SemaphoreType.DMA((N_SEND,)),
            pltpu.SemaphoreType.DMA((N_RECV,)),
            pltpu.SemaphoreType.DMA((N_LOCAL,)),
        ],
        compiler_params=pltpu.CompilerParams(
            collective_id=0, has_side_effects=True, vmem_limit_bytes=53 * 2**20
        ),
        cost_estimate=pl.CostEstimate(flops=10_500_000_000, bytes_accessed=12_000_000, transcendentals=6_300_000),
    )(queries, keys, values, stream, out_weight.reshape(3, HD, D), norm_gain.reshape(1, D), up_weight)


def solution(mesh):
    in_specs = (
        P("seq", "tensor"),
        P("seq", "tensor"),
        P("seq", "tensor"),
        P("seq", "tensor"),
        P("tensor", None),
        P(),
        P("seq", "tensor"),
    )
    out_specs = (P("seq", "tensor"), P("seq", "tensor"))
    return jax.shard_map(body, mesh=mesh, in_specs=in_specs, out_specs=out_specs, check_vma=False)
```

time: 119 us -> 110 us (0.924)
  Pallas kernels: 114 us -> 107 us
  local copies, waits for them, and re-layouts: 3.84 us -> 1.63 us
    pallas_call x1, Pallas kernels: 114 us -> 107 us  [body(): pl.pallas_call(kernel, out_shape=(pltpu.VMEM((ROWS, OWN), BF16), pltpu.VM...]
    unnamed x2, local copies, waits for them, and re-layouts: 3.84 us -> 1.63 us
where the time goes in v3:
time: 110 us
  Pallas kernels  107 us (97%)
  local copies, waits for them, and re-layouts  1.63 us (1%)
    pallas_call x1, Pallas kernels, body(): pl.pallas_call(kernel, out_shape=(pltpu.VMEM((ROWS, OWN), BF16), pltpu.VM...  107 us

profile of v3, /device:TPU:1, one launch (start us, length us, event | category | flops | bytes accessed | tf_op | source)
XLA Modules:
  0.0 109.8 jit_solution(4088197913438744415)
XLA Ops:
  0.6 107.5 %shard_map.86 = (bf16[512,384]{1,0:T(8,128)(2,1)S(1)}, bf16[512,768]{1,0:T(8,128)(2,1)S(1)}) custom-call(bf16[512,384]{1,0:T(8,128)(2,1)} %q_ref.1, bf16[512,384]{1,0:T(8,128)(2,1)} %k_ref.1, bf16[512,384]{1,0:T(8,128)(2,1)} %v_ref.1, bf16[512,384]{1,0:T(8,128)(2,1)} %stream_ref.1, bf16[3,128,6144]{2,1,0:T(8,128)(2,1)} %bitcast.2, f32[1,6144]{1,0:T(1,128)} %bitcast.3, ...), custom_call_target="tpu_custom_call" | custom-call | flops 10499999744 | bytes 12000000 | tf_op jit(solution)/shard_map/pallas_call | solution.py:484
  108.1 0.7 copy.11
  108.9 0.9 copy.12

commit v4 on v3

--- a/solution.py
+++ b/solution.py
@@ -16,6 +16,7 @@
 
 ROWS = 512
 HALF = 256
+QUARTER = 128
 OWN = 384
 WIDE = 768
 SPLIT = 512
@@ -63,8 +64,8 @@
             self.free.append(self.slots.pop(name))
 
 
-N_SEND = 47
-N_RECV = 66
+N_SEND = 53
+N_RECV = 75
 N_LOCAL = 8
 
 
@@ -244,7 +245,6 @@
     go.arrive_all("f1", kvb.at[1, 3], zp)
     attend_far(1, 1)
     give_back(1)
-    attend_far(0, 1)
     go.arrive_all("f2", kvb.at[2, 3], zp)
     attend_far(1, 2, 0)
     give_back(2, "a", lower)
@@ -253,6 +253,7 @@
     cross(6)
     cross(8)
     cross(10)
+    attend_far(0, 1)
     attend_far(0, 2)
 
     def merge(h, rows):
@@ -273,7 +274,12 @@
         go.arrive(f"s{h}", f"o{h}")
         merge(h, whole)
         go(f"att{h}", att.at[h, :, own_half], att.at[h, :, own_half], cp, "att")
-    go.drain(*[f"{kind}{h}" for kind in ("n+", "n-", "f+", "f-", "q") for h in range(3)], *[f"ow{j}" for j in range(8)])
+    go.drain(*[f"{kind}{h}" for kind in ("n+", "n-") for h in range(2)], "f+0", "f-0", "q0", "q1", "q2")
+    go.drain(*[f"ow{j}" for j in range(8)])
+    for part, rows in (("a", lower), ("b", upper)):
+        go.arrive(f"s2{part}", f"o2{part}")
+        merge(2, rows)
+        go(f"att2{part}", att.at[2, rows, own_half], att.at[2, rows, own_half], cp)
     landed(5, owb.at[:, :, c])
     go.arrive_all("ow", owb.at[:, :, 1 - c], cp)
     go.arrive_all("att", att.at[0:2, :, own_half], cp)
@@ -290,120 +296,123 @@
             att[2, rows, :], owb[chip(dy, dx), 2].reshape(2 * HD, OWN), preferred_element_type=F32
         )
 
-    p_far[1] = project_two(1, 2)
-    p_plus[1] = project_two(1, 1)
-    p_minus[1] = project_two(1, -1)
-    for part, rows in (("a", lower), ("b", upper)):
-        go.arrive(f"s2{part}", f"o2{part}")
-        merge(2, rows)
-        go(f"att2{part}", att.at[2, rows, own_half], att.at[2, rows, own_half], cp)
-    p_far[0] = project_two(0, 2)
     before, after, across = token_block(-1, 0), token_block(1, 0), token_block(2, 0)
     opposite = token_block(0, 1)
     before_opposite, after_opposite, across_opposite = token_block(-1, 1), token_block(1, 1), token_block(2, 1)
 
-    def send_far(dy, rows):
-        p_out[dy, rows, :] = (p_far[dy, rows, :] + project_last(dy, 2, rows)).astype(BF16)
-        if rows is lower:
-            go(f"far+{dy}", p_out.at[dy, rows], r_far.at[dy, rows], xp)
+    def quarters(a):
+        return a.reshape(2, 2, QUARTER, OWN)
+
+    def send_far(dy, half):
+        go(f"far+{dy}{half}", p_out.at[dy, half, 0], r_far.at[dy, half, 0], xp, f"far+{dy}")
+        go(f"far-{dy}{half}", p_out.at[dy, half, 1], r_far.at[dy, half, 1], xm, f"far-{dy}")
+
+    def far_block(dy, rows, half):
+        out = p_far[dy, rows, :] + project_last(dy, 2, rows)
+        p_out[dy, half] = out.astype(BF16).reshape(2, QUARTER, OWN)
+
+    def near_blocks(dy):
+        p_plus[dy] = quarters(project_two(dy, 1) + project_last(dy, 1, whole))
+        y_out[0, dy, :, 1] = p_plus[dy, :, 1].astype(BF16)
+        p_minus[dy] = quarters(project_two(dy, -1) + project_last(dy, -1, whole))
+        y_out[1, dy, :, 0] = p_minus[dy, :, 0].astype(BF16)
+
+    def send_early(dy):
+        go(f"early+{dy}", y_out.at[0, dy, :, 1], r_plus.at[dy, :, 1], xp, f"plus{dy}")
+        go(f"early-{dy}", y_out.at[1, dy, :, 0], r_minus.at[dy, :, 0], xm, f"minus{dy}")
+
+    def add_far(dy):
+        go.arrive_all(f"far+{dy}", r_far.at[dy, :, 0], xp)
+        y_out[0, dy, :, 0] = (p_plus[dy, :, 0] + r_far[dy, :, 0].astype(F32)).astype(BF16)
+        if dy == 1:
+            go("late+1", y_out.at[0, 1, :, 0], r_plus.at[1, :, 0], xp, "plus1")
         else:
-            go(f"far-{dy}", p_out.at[dy, rows], r_far.at[dy, rows], xm)
-
-    def near_blocks(dy):
-        p_plus[dy] += project_last(dy, 1, whole)
-        y_out[0, dy, upper, :] = p_plus[dy, upper, :].astype(BF16)
-        p_minus[dy] += project_last(dy, -1, whole)
-        y_out[1, dy, lower, :] = p_minus[dy, lower, :].astype(BF16)
-
-    def send_early(dy):
-        go(f"early+{dy}", y_out.at[0, dy, upper], r_plus.at[dy, upper], xp, f"plus{dy}")
-        go(f"early-{dy}", y_out.at[1, dy, lower], r_minus.at[dy, lower], xm, f"minus{dy}")
-
-    def send_late(dy):
-        go.arrive(f"far+{dy}")
-        y_out[0, dy, lower, :] = (p_plus[dy, lower, :] + r_far[dy, lower, :].astype(F32)).astype(BF16)
-        go(f"late+{dy}", y_out.at[0, dy, lower], r_plus.at[dy, lower], xp, f"plus{dy}")
-        go.arrive(f"far-{dy}")
-        y_out[1, dy, upper, :] = (p_minus[dy, upper, :] + r_far[dy, upper, :].astype(F32)).astype(BF16)
-        go(f"late-{dy}", y_out.at[1, dy, upper], r_minus.at[dy, upper], xm, f"minus{dy}")
-
-    def near_sum(dy):
-        go.arrive_all(f"plus{dy}", r_plus.at[dy], xp)
-        go.arrive_all(f"minus{dy}", r_minus.at[dy], xm)
-        return p_here[dy] + r_plus[dy].astype(F32) + r_minus[dy].astype(F32)
-
+            for half in (0, 1):
+                go(f"late+0{half}", y_out.at[0, 0, half, 0], r_plus.at[0, half, 0], xp)
+        go.arrive_all(f"far-{dy}", r_far.at[dy, :, 1], xm)
+        y_out[1, dy, :, 1] = (p_minus[dy, :, 1] + r_far[dy, :, 1].astype(F32)).astype(BF16)
+        if dy == 1:
+            go("late-1", y_out.at[1, 1, :, 1], r_minus.at[1, :, 1], xm, "minus1")
+        else:
+            for half in (0, 1):
+                go(f"late-0{half}", y_out.at[1, 0, half, 1], r_minus.at[0, half, 1], xm)
+
+    p_far[1] = project_two(1, 2)
     go.arrive("att2a")
-    send_far(1, lower)
+    far_block(1, lower, 0)
+    send_far(1, 0)
     go.arrive("att2b")
-    send_far(1, upper)
+    far_block(1, upper, 1)
+    send_far(1, 1)
     near_blocks(1)
     send_early(1)
     go.arrive("wz2+")
     go("wq1", wb.at[before, second], wb.at[before, second], yp)
     go.arrive("wz2-")
     go("wf2", wb.at[after, second], wb.at[after, second], zm)
-    p_plus[0] = project_two(0, 1)
-    p_minus[0] = project_two(0, -1)
+    go.arrive_all("wy1", wb.at[opposite, first], yp)
+    q1, q2 = pl.ds(0, SPLIT // 2), pl.ds(SPLIT // 2, SPLIT // 2)
+    go("wp+a", wb.at[opposite, q1], wb.at[opposite, q1], zp)
+    p_far[0] = project_two(0, 2)
+    far_block(0, lower, 0)
+    far_block(0, upper, 1)
     near_blocks(0)
-    send_late(1)
-    send_far(0, lower)
-    send_far(0, upper)
+    add_far(1)
+    send_far(0, 0)
+    send_far(0, 1)
     send_early(0)
     for dy in (1, 0):
         p_here[dy] = project_two(dy, 0) + project_last(dy, 0, whole)
-    go.arrive_all("wy1", wb.at[opposite, first], yp)
-    go("wp+", wb.at[opposite, first], wb.at[opposite, first], zp)
-    go("wp-", wb.at[opposite, first], wb.at[opposite, first], zm)
-    y_in[0] = near_sum(1).astype(BF16)
+    go.drain("n+2", "n-2", "f+1", "f-1", "f+2", "f-2", "s0", "o0", "s1", "o1", "att0", "att1")
+    go.arrive_all("plus1", r_plus.at[1], xp)
+    go.arrive_all("minus1", r_minus.at[1], xm)
+    near = p_here[1] + (r_plus[1].astype(F32) + r_minus[1].astype(F32)).reshape(ROWS, OWN)
+    y_in[0] = near.astype(BF16)
     go("rows", y_in.at[0], y_in.at[1], yq)
-    half1, half2 = pl.ds(SPLIT, 128), pl.ds(SPLIT + 128, 128)
-    go("wq2a", wb.at[after, half1], wb.at[after, half1], yp, "wq2")
-    send_late(0)
+    chunk1, chunk2 = pl.ds(SPLIT, 64), pl.ds(SPLIT + 64, WIDE - SPLIT - 64)
+    go("wq2a", wb.at[after, chunk1], wb.at[after, chunk1], yp, "wq2")
     rows1, rows2 = pl.ds(0, WIDE // 2), pl.ds(WIDE // 2, SPLIT - WIDE // 2)
     go.arrive("wz1+")
     go("wf1", wb.at[before, rows1], wb.at[before, rows1], zp, "wf")
     go.arrive("wz1-")
     go("wf3", wb.at[after, rows2], wb.at[after, rows2], zm, "wf")
+    go("wp-a", wb.at[opposite, q2], wb.at[opposite, q2], zm)
+    go("wp+b", wb.at[opposite, q2], wb.at[opposite, q2], zp)
+    go("wp-b", wb.at[opposite, q1], wb.at[opposite, q1], zm)
+    add_far(0)
     landed(6, stream_vm)
-    here = near_sum(0) + stream_vm[...].astype(F32)
-    go.arrive("rows")
-    own = chip(0, 0)
-    residual = (here + y_in[1].astype(F32)).astype(BF16)
-    xb[own, :, mine] = residual
-    residual_ref[...] = residual
-
-    def block(j, rows=slice(None)):
-        return xb.at[j, rows, mine]
-
-    def spread(dy):
+    own, other_chip = chip(0, 0), chip(1, 0)
+
+    def block(j, half=slice(None), way=slice(None)):
+        return xb.at[j, half, way, :, mine]
+
+    def spread(dy, half):
         j = chip(dy, 0)
-        go(f"x+{dy}a", block(j, lower), block(j, lower), xp)
-        go(f"x-{dy}a", block(j, upper), block(j, upper), xm)
-        go(f"x+{dy}b", block(j, upper), block(j, upper), xp)
-        go(f"x-{dy}b", block(j, lower), block(j, lower), xm)
-
-    def pass_on(dy):
-        left, right = chip(dy, -1), chip(dy, 1)
-        go.arrive(f"x+{dy}a")
-        go(f"xf+{dy}", block(left, lower), block(left, lower), xp, f"xf{dy}")
-        go.arrive(f"x-{dy}a")
-        go(f"xf-{dy}", block(right, upper), block(right, upper), xm, f"xf{dy}")
+        go(f"x+{dy}{half}", block(j, half), block(j, half), xp)
+        go(f"x-{dy}{half}", block(j, half), block(j, half), xm)
 
     def pass_core(dy):
         left, right = chip(dy, -1), chip(dy, 1)
-        go.arrive(f"x+{dy}b")
         go(f"xc+{dy}", block(left), block(left), cp)
-        go.arrive(f"x-{dy}b")
         go(f"xc-{dy}", block(right), block(right), cp)
 
-    def pass_far(dy):
-        j = chip(dy, 2)
-        go.arrive_all(f"xf{dy}", block(j), xp)
-        go(f"xcf{dy}", block(j), block(j), cp)
+    go.arrive_all("plus0", r_plus.at[0, :, 1], xp)
+    go.arrive_all("minus0", r_minus.at[0, :, 0], xm)
+    for half, rows in ((0, lower), (1, upper)):
+        go.arrive(f"late+0{half}", f"late-0{half}")
+        if half == 0:
+            go.arrive("rows")
+        here = p_here[0, rows, :] + (r_plus[0, half].astype(F32) + r_minus[0, half].astype(F32)).reshape(HALF, OWN)
+        here = here + stream_vm[rows].astype(F32) + y_in[1, rows].astype(F32)
+        residual = here.astype(BF16)
+        xb[own, half, :, :, mine] = residual.reshape(2, QUARTER, OWN)
+        residual_ref[rows] = residual
+        spread(0, half)
+        go(f"xy{half}", block(own, half), block(own, half), yq)
 
     def prepare(j, start=False):
         gain = gain_ref[:, pl.ds(pl.multiple_of(j * WIDE, 128), WIDE)]
-        level = xb[j].astype(F32)
+        level = xb[j].reshape(ROWS, WIDE).astype(F32)
         xg[j] = (level * gain).astype(BF16)
         level = level * level
         sums = level[:, 0:128]
@@ -415,65 +424,95 @@
         product = jnp.dot(xg[j], wb[j], preferred_element_type=F32)
         total[...] = product if start else total[...] + product
 
-    go.drain(*[f"{kind}{sign}{dy}" for kind in ("far", "early", "late") for sign in "+-" for dy in (0, 1)])
-    go.drain(*"s0 o0 s1 o1 s2a o2a s2b o2b att0 att1 att2a att2b wy0 wy2 wy4 wy6 wy8 wy10".split())
-    go.drain("wz2+", "wz2-", "wz1+", "wz1-")
-    spread(0)
-    go("xy", block(own), block(own), yq)
     go("xc", block(own), block(own), cp)
-    go("wq2b", wb.at[after, half2], wb.at[after, half2], yp, "wq2")
+    go("wq2b", wb.at[after, chunk2], wb.at[after, chunk2], yp, "wq2")
     go.arrive("wf2")
     go("wq3", wb.at[across, second], wb.at[across, second], yp)
+    go.drain(*[f"early{sign}{dy}" for sign in "+-" for dy in (0, 1)])
+    go.drain(*[f"far{sign}{dy}{half}" for sign in "+-" for dy in (0, 1) for half in (0, 1)])
+    go.drain("s2a", "o2a", "s2b", "o2b", "att2a", "att2b", *[f"wy{i}" for i in range(0, 12, 2)])
+    go.drain("wz2+", "wz2-", "wz1+", "wz1-", "late+1", "late-1")
+    go.arrive("xy0")
+    spread(1, 0)
     go.arrive("xc")
     prepare(own, start=True)
-    pass_on(0)
+    go.arrive("xy1")
+    spread(1, 1)
+    go("xcy", block(other_chip), block(other_chip), cp)
+    go.arrive("x+00", "x+01")
+    go("xf+0", block(chip(0, -1), way=0), block(chip(0, -1), way=0), xp, "xf0")
+    go.arrive("x-00", "x-01")
+    go("xf-0", block(chip(0, 1), way=1), block(chip(0, 1), way=1), xm, "xf0")
     pass_core(0)
-    go.arrive("xy")
-    spread(1)
-    other_chip = chip(1, 0)
-    go("xcy", block(other_chip), block(other_chip), cp)
-    q1, q2 = pl.ds(0, SPLIT // 2), pl.ds(SPLIT // 2, SPLIT // 2)
-    go.arrive("wp+")
+    go.arrive("wp+a")
     go("wpf+", wb.at[before_opposite, q1], wb.at[before_opposite, q1], zp, "wpf")
-    go.arrive("wp-")
+    go.arrive("wp-a")
     go("wpf-", wb.at[after_opposite, q2], wb.at[after_opposite, q2], zm, "wpf")
     go.arrive("xc+0")
     prepare(chip(0, -1))
     go.arrive("xc-0")
     prepare(chip(0, 1))
-    pass_far(0)
     go.arrive("xcy")
     prepare(other_chip)
-    pass_on(1)
-    go.arrive("xcf0")
-    prepare(chip(0, 2))
-    go.arrive_all("wf", wb.at[across, first], zp)
+
+    def pass_far(half):
+        go.arrive(f"x+1{half}")
+        go(f"xf+1{half}", block(chip(1, -1), half, 0), block(chip(1, -1), half, 0), xp, f"xf1{half}")
+        go.arrive(f"x-1{half}")
+        go(f"xf-1{half}", block(chip(1, 1), half, 1), block(chip(1, 1), half, 1), xm, f"xf1{half}")
+
     same = lax.rem(x + yh, 2)
     rest = 1 - same
+    far_chip, last_chip = chip(0, 2), chip(1, 2)
+    order = [
+        chip(0, rest),
+        jnp.where(same == 0, chip(0, 3), other_chip),
+        chip(1, 1),
+        chip(1, 3),
+        far_chip,
+    ]
+    passed = order[0] == across_opposite
+    turn = []
+    for k in range(4):
+        turn.append(jnp.where(passed, order[k + 1], order[k]))
+        passed = passed | (order[k + 1] == across_opposite)
+    turn.append(jnp.where(passed, across_opposite, order[4]))
+    go.arrive_all("wf", wb.at[across, first], zp)
     expand(chip(0, same), start=True)
-    expand(chip(0, same + 2))
+    pass_far(0)
+    expand(jnp.where(same == 0, other_chip, chip(0, 3)))
     go.arrive_all("wy2", wb.at[opposite, second], yp)
-    go.arrive("wq1", "wq3")
+    go.arrive("wq1", "wp+b", "wp-b")
     go.arrive_all("wq2", wb.at[after_opposite, second], yp)
-    go.arrive_all("wpf", wb.at[across_opposite, first], zp)
-    expand(chip(0, rest))
+    expand(turn[0])
+    pass_far(1)
     pass_core(1)
-    expand(chip(0, rest + 2))
     go.arrive("xc+1")
     prepare(chip(1, -1))
     go.arrive("xc-1")
     prepare(chip(1, 1))
-    expand(other_chip)
-    expand(chip(1, 1))
-    pass_far(1)
-    expand(chip(1, -1))
-    go.arrive("xcf1")
-    prepare(chip(1, 2))
-    expand(chip(1, 2))
-
-    for rows in (lower, upper):
-        inverse = lax.rsqrt(jnp.sum(squares[rows], axis=1, keepdims=True) * (1.0 / D) + 1e-6)
-        expanded_ref[rows] = jax.nn.gelu(total[rows] * inverse, approximate=True).astype(BF16)
+    expand(turn[1])
+    go.arrive_all("xf0", block(far_chip), xp)
+    go("xcf0", block(far_chip), block(far_chip), cp)
+    expand(turn[2])
+    go.arrive("xcf0")
+    prepare(far_chip)
+    go.arrive_all("xf10", block(last_chip, 0), xp)
+    go("xcf10", block(last_chip, 0), block(last_chip, 0), cp)
+    expand(turn[3])
+    go.arrive_all("xf11", block(last_chip, 1), xp)
+    go("xcf11", block(last_chip, 1), block(last_chip, 1), cp)
+    go.arrive("wq3")
+    go.arrive_all("wpf", wb.at[across_opposite, first], zp)
+    expand(turn[4])
+    gain = gain_ref[:, pl.ds(pl.multiple_of(last_chip * WIDE, 128), WIDE)]
+    for half, rows in ((0, lower), (1, upper)):
+        go.arrive(f"xcf1{half}")
+        level = xb[last_chip, half].reshape(HALF, WIDE).astype(F32)
+        product = jnp.dot((level * gain).astype(BF16), wb[last_chip], preferred_element_type=F32)
+        square = jnp.sum(level * level, axis=1, keepdims=True) + jnp.sum(squares[rows], axis=1, keepdims=True)
+        inverse = lax.rsqrt(square * (1.0 / D) + 1e-6)
+        expanded_ref[rows] = jax.nn.gelu((total[rows] + product) * inverse, approximate=True).astype(BF16)
     go.drain()
     assert go.used <= N_SEND and len(go.groups) <= N_RECV, (go.used, len(go.groups))
 
@@ -503,16 +542,16 @@
             pltpu.VMEM((8, WIDE, WIDE), BF16),
             pltpu.VMEM((ROWS, OWN), BF16),
             pltpu.VMEM((2, ROWS, OWN), F32),
+            pltpu.VMEM((2, 2, 2, QUARTER, OWN), BF16),
+            pltpu.VMEM((2, 2, 2, QUARTER, OWN), F32),
+            pltpu.VMEM((2, 2, 2, QUARTER, OWN), F32),
+            pltpu.VMEM((2, ROWS, OWN), F32),
+            pltpu.VMEM((2, 2, 2, QUARTER, OWN), BF16),
+            pltpu.VMEM((2, 2, 2, QUARTER, OWN), BF16),
+            pltpu.VMEM((2, 2, 2, QUARTER, OWN), BF16),
+            pltpu.VMEM((2, 2, 2, 2, QUARTER, OWN), BF16),
             pltpu.VMEM((2, ROWS, OWN), BF16),
-            pltpu.VMEM((2, ROWS, OWN), F32),
-            pltpu.VMEM((2, ROWS, OWN), F32),
-            pltpu.VMEM((2, ROWS, OWN), F32),
-            pltpu.VMEM((2, ROWS, OWN), BF16),
-            pltpu.VMEM((2, ROWS, OWN), BF16),
-            pltpu.VMEM((2, ROWS, OWN), BF16),
-            pltpu.VMEM((2, 2, ROWS, OWN), BF16),
-            pltpu.VMEM((2, ROWS, OWN), BF16),
-            pltpu.VMEM((8, ROWS, WIDE), BF16),
+            pltpu.VMEM((8, 2, 2, QUARTER, WIDE), BF16),
             pltpu.VMEM((8, ROWS, WIDE), BF16),
             pltpu.VMEM((ROWS, WIDE), F32),
             pltpu.VMEM((ROWS, 128), F32),

time: 110 us -> 106 us (0.964)
  Pallas kernels: 107 us -> 103 us
    pallas_call x1, Pallas kernels: 107 us -> 103 us  [body(): pl.pallas_call(kernel, out_shape=(pltpu.VMEM((ROWS, OWN), BF16), pltpu.VM...]
where the time goes in v4:
time: 106 us; the launch traced here: 105 us
  Pallas kernels  103 us (97%)
  local copies, waits for them, and re-layouts  1.63 us (2%)
    pallas_call x1, Pallas kernels, body(): pl.pallas_call(kernel, out_shape=(pltpu.VMEM((ROWS, OWN), BF16), pltpu.VM...  103 us

profile of v4, /device:TPU:1, one launch (start us, length us, event | category | flops | bytes accessed | tf_op | source)
XLA Modules:
  0.0 105.4 jit_solution(5356288954317136602)
XLA Ops:
  0.6 103.1 %shard_map.86 = (bf16[512,384]{1,0:T(8,128)(2,1)S(1)}, bf16[512,768]{1,0:T(8,128)(2,1)S(1)}) custom-call(bf16[512,384]{1,0:T(8,128)(2,1)} %q_ref.1, bf16[512,384]{1,0:T(8,128)(2,1)} %k_ref.1, bf16[512,384]{1,0:T(8,128)(2,1)} %v_ref.1, bf16[512,384]{1,0:T(8,128)(2,1)} %stream_ref.1, bf16[3,128,6144]{2,1,0:T(8,128)(2,1)} %bitcast.2, f32[1,6144]{1,0:T(1,128)} %bitcast.3, ...), custom_call_target="tpu_custom_call" | custom-call | flops 10499999744 | bytes 12000000 | tf_op jit(solution)/shard_map/pallas_call | solution.py:523
  103.8 0.7 copy.11
  104.5 0.9 copy.12

commit v5 on v4

--- a/solution.py
+++ b/solution.py
@@ -64,7 +64,7 @@
             self.free.append(self.slots.pop(name))
 
 
-N_SEND = 53
+N_SEND = 54
 N_RECV = 75
 N_LOCAL = 8
 
@@ -220,6 +220,7 @@
 
     cross(0)
     cross(2)
+    cross(4, 1)
     far(0)
     near(2)
     go.arrive("q0")
@@ -232,16 +233,17 @@
     go.arrive_all("f0", kvb.at[0, 3], zp)
     attend_far(1, 0)
     give_back(0)
-    cross(4)
+    cross(5)
+    cross(7, 1)
     attend_far(0, 0)
     far(2)
+    go.arrive("q2")
+    attend_near(1, 2)
+    attend_near(0, 2)
     go("wz2+", wb.at[own_rows, second], wb.at[own_rows, second], zp)
     go("wz2-", wb.at[own_rows, second], wb.at[own_rows, second], zm)
     go("wz1+", wb.at[own_rows, first], wb.at[own_rows, first], zp)
     go("wz1-", wb.at[own_rows, first], wb.at[own_rows, first], zm)
-    go.arrive("q2")
-    attend_near(1, 2)
-    attend_near(0, 2)
     go.arrive_all("f1", kvb.at[1, 3], zp)
     attend_far(1, 1)
     give_back(1)
@@ -250,9 +252,6 @@
     give_back(2, "a", lower)
     attend_far(1, 2, 1)
     give_back(2, "b", upper)
-    cross(6)
-    cross(8)
-    cross(10)
     attend_far(0, 1)
     attend_far(0, 2)
 
@@ -280,6 +279,8 @@
         go.arrive(f"s2{part}", f"o2{part}")
         merge(2, rows)
         go(f"att2{part}", att.at[2, rows, own_half], att.at[2, rows, own_half], cp)
+    cross(8)
+    cross(10)
     landed(5, owb.at[:, :, c])
     go.arrive_all("ow", owb.at[:, :, 1 - c], cp)
     go.arrive_all("att", att.at[0:2, :, own_half], cp)
@@ -430,7 +431,7 @@
     go("wq3", wb.at[across, second], wb.at[across, second], yp)
     go.drain(*[f"early{sign}{dy}" for sign in "+-" for dy in (0, 1)])
     go.drain(*[f"far{sign}{dy}{half}" for sign in "+-" for dy in (0, 1) for half in (0, 1)])
-    go.drain("s2a", "o2a", "s2b", "o2b", "att2a", "att2b", *[f"wy{i}" for i in range(0, 12, 2)])
+    go.drain("s2a", "o2a", "s2b", "o2b", "att2a", "att2b", *[f"wy{i}" for i in (0, 2, 4, 5, 7, 8, 10)])
     go.drain("wz2+", "wz2-", "wz1+", "wz1-", "late+1", "late-1")
     go.arrive("xy0")
     spread(1, 0)

time: 106 us -> 106 us (level)
  no operation moved by 1% of the time
where the time goes in v5:
time: 106 us; the launch traced here: 105 us
  Pallas kernels  103 us (97%)
  local copies, waits for them, and re-layouts  1.63 us (2%)
    pallas_call x1, Pallas kernels, body(): pl.pallas_call(kernel, out_shape=(pltpu.VMEM((ROWS, OWN), BF16), pltpu.VM...  103 us

profile of v5, /device:TPU:1, one launch (start us, length us, event | category | flops | bytes accessed | tf_op | source)
XLA Modules:
  0.0 105.4 jit_solution(15453249230860041114)
XLA Ops:
  0.6 103.1 %shard_map.86 = (bf16[512,384]{1,0:T(8,128)(2,1)S(1)}, bf16[512,768]{1,0:T(8,128)(2,1)S(1)}) custom-call(bf16[512,384]{1,0:T(8,128)(2,1)} %q_ref.1, bf16[512,384]{1,0:T(8,128)(2,1)} %k_ref.1, bf16[512,384]{1,0:T(8,128)(2,1)} %v_ref.1, bf16[512,384]{1,0:T(8,128)(2,1)} %stream_ref.1, bf16[3,128,6144]{2,1,0:T(8,128)(2,1)} %bitcast.2, f32[1,6144]{1,0:T(1,128)} %bitcast.3, ...), custom_call_target="tpu_custom_call" | custom-call | flops 10499999744 | bytes 12000000 | tf_op jit(solution)/shard_map/pallas_call | solution.py:524
  103.8 0.7 copy.11
  104.5 0.9 copy.12

commit v6 on v5

--- a/solution.py
+++ b/solution.py
@@ -65,6 +65,8 @@
 
 
 N_SEND = 54
+EARLY = 384
+AHEAD = 160
 N_RECV = 75
 N_LOCAL = 8
 
@@ -214,13 +216,12 @@
     first, second = pl.ds(0, SPLIT), pl.ds(SPLIT, WIDE - SPLIT)
     own_rows = token_block(0, 0)
 
-    def cross(i, n=2):
-        rows = pl.ds(i * 64, n * 64)
-        go(f"wy{i}", wb.at[own_rows, rows], wb.at[own_rows, rows], yp, "wy1" if i < SPLIT // 64 else "wy2")
-
-    cross(0)
-    cross(2)
-    cross(4, 1)
+    def cross(start, stop):
+        rows = pl.ds(start, stop - start)
+        go(f"wy{start}", wb.at[own_rows, rows], wb.at[own_rows, rows], yp, "wy1" if start < SPLIT else "wy2")
+
+    cross(0, 128)
+    cross(128, 256)
     far(0)
     near(2)
     go.arrive("q0")
@@ -233,8 +234,7 @@
     go.arrive_all("f0", kvb.at[0, 3], zp)
     attend_far(1, 0)
     give_back(0)
-    cross(5)
-    cross(7, 1)
+    cross(256, EARLY)
     attend_far(0, 0)
     far(2)
     go.arrive("q2")
@@ -279,8 +279,9 @@
         go.arrive(f"s2{part}", f"o2{part}")
         merge(2, rows)
         go(f"att2{part}", att.at[2, rows, own_half], att.at[2, rows, own_half], cp)
-    cross(8)
-    cross(10)
+    cross(EARLY, SPLIT)
+    cross(SPLIT, 640)
+    cross(640, WIDE)
     landed(5, owb.at[:, :, c])
     go.arrive_all("ow", owb.at[:, :, 1 - c], cp)
     go.arrive_all("att", att.at[0:2, :, own_half], cp)
@@ -348,12 +349,10 @@
     near_blocks(1)
     send_early(1)
     go.arrive("wz2+")
-    go("wq1", wb.at[before, second], wb.at[before, second], yp)
+    part1, part2 = pl.ds(SPLIT, AHEAD), pl.ds(SPLIT + AHEAD, WIDE - SPLIT - AHEAD)
+    go("wq1a", wb.at[before, part1], wb.at[before, part1], yp, "wq1")
     go.arrive("wz2-")
     go("wf2", wb.at[after, second], wb.at[after, second], zm)
-    go.arrive_all("wy1", wb.at[opposite, first], yp)
-    q1, q2 = pl.ds(0, SPLIT // 2), pl.ds(SPLIT // 2, SPLIT // 2)
-    go("wp+a", wb.at[opposite, q1], wb.at[opposite, q1], zp)
     p_far[0] = project_two(0, 2)
     far_block(0, lower, 0)
     far_block(0, upper, 1)
@@ -364,14 +363,16 @@
     send_early(0)
     for dy in (1, 0):
         p_here[dy] = project_two(dy, 0) + project_last(dy, 0, whole)
+    go.arrive_all("wy1", wb.at[opposite, first], yp)
+    q1, q2 = pl.ds(0, SPLIT // 2), pl.ds(SPLIT // 2, SPLIT // 2)
+    go("wp+a", wb.at[opposite, q1], wb.at[opposite, q1], zp)
     go.drain("n+2", "n-2", "f+1", "f-1", "f+2", "f-2", "s0", "o0", "s1", "o1", "att0", "att1")
     go.arrive_all("plus1", r_plus.at[1], xp)
     go.arrive_all("minus1", r_minus.at[1], xm)
     near = p_here[1] + (r_plus[1].astype(F32) + r_minus[1].astype(F32)).reshape(ROWS, OWN)
     y_in[0] = near.astype(BF16)
     go("rows", y_in.at[0], y_in.at[1], yq)
-    chunk1, chunk2 = pl.ds(SPLIT, 64), pl.ds(SPLIT + 64, WIDE - SPLIT - 64)
-    go("wq2a", wb.at[after, chunk1], wb.at[after, chunk1], yp, "wq2")
+    go("wq1b", wb.at[before, part2], wb.at[before, part2], yp, "wq1")
     rows1, rows2 = pl.ds(0, WIDE // 2), pl.ds(WIDE // 2, SPLIT - WIDE // 2)
     go.arrive("wz1+")
     go("wf1", wb.at[before, rows1], wb.at[before, rows1], zp, "wf")
@@ -426,12 +427,12 @@
         total[...] = product if start else total[...] + product
 
     go("xc", block(own), block(own), cp)
-    go("wq2b", wb.at[after, chunk2], wb.at[after, chunk2], yp, "wq2")
+    go("wq2", wb.at[after, second], wb.at[after, second], yp)
     go.arrive("wf2")
     go("wq3", wb.at[across, second], wb.at[across, second], yp)
     go.drain(*[f"early{sign}{dy}" for sign in "+-" for dy in (0, 1)])
     go.drain(*[f"far{sign}{dy}{half}" for sign in "+-" for dy in (0, 1) for half in (0, 1)])
-    go.drain("s2a", "o2a", "s2b", "o2b", "att2a", "att2b", *[f"wy{i}" for i in (0, 2, 4, 5, 7, 8, 10)])
+    go.drain("s2a", "o2a", "s2b", "o2b", "att2a", "att2b", *[f"wy{i}" for i in (0, 128, 256, EARLY, SPLIT, 640)])
     go.drain("wz2+", "wz2-", "wz1+", "wz1-", "late+1", "late-1")
     go.arrive("xy0")
     spread(1, 0)
@@ -482,20 +483,20 @@
     expand(chip(0, same), start=True)
     pass_far(0)
     expand(jnp.where(same == 0, other_chip, chip(0, 3)))
-    go.arrive_all("wy2", wb.at[opposite, second], yp)
-    go.arrive("wq1", "wp+b", "wp-b")
-    go.arrive_all("wq2", wb.at[after_opposite, second], yp)
-    expand(turn[0])
     pass_far(1)
     pass_core(1)
     go.arrive("xc+1")
     prepare(chip(1, -1))
     go.arrive("xc-1")
     prepare(chip(1, 1))
+    go.arrive_all("wy2", wb.at[opposite, second], yp)
+    go.arrive_all("wq1", wb.at[before_opposite, second], yp)
+    go.arrive("wp+b", "wp-b", "wq2")
+    expand(turn[0])
     expand(turn[1])
+    expand(turn[2])
     go.arrive_all("xf0", block(far_chip), xp)
     go("xcf0", block(far_chip), block(far_chip), cp)
-    expand(turn[2])
     go.arrive("xcf0")
     prepare(far_chip)
     go.arrive_all("xf10", block(last_chip, 0), xp)

time: 106 us -> 103 us (0.972)
  Pallas kernels: 103 us -> 101 us
    pallas_call x1, Pallas kernels: 103 us -> 101 us  [body(): pl.pallas_call(kernel, out_shape=(pltpu.VMEM((ROWS, OWN), BF16), pltpu.VM...]
where the time goes in v6:
time: 103 us
  Pallas kernels  101 us (98%)
  local copies, waits for them, and re-layouts  1.63 us (2%)
    pallas_call x1, Pallas kernels, body(): pl.pallas_call(kernel, out_shape=(pltpu.VMEM((ROWS, OWN), BF16), pltpu.VM...  101 us

profile of v6, /device:TPU:1, one launch (start us, length us, event | category | flops | bytes accessed | tf_op | source)
XLA Modules:
  0.0 103.3 jit_solution(17739260146836616903)
XLA Ops:
  0.6 101.1 %shard_map.86 = (bf16[512,384]{1,0:T(8,128)(2,1)S(1)}, bf16[512,768]{1,0:T(8,128)(2,1)S(1)}) custom-call(bf16[512,384]{1,0:T(8,128)(2,1)} %q_ref.1, bf16[512,384]{1,0:T(8,128)(2,1)} %k_ref.1, bf16[512,384]{1,0:T(8,128)(2,1)} %v_ref.1, bf16[512,384]{1,0:T(8,128)(2,1)} %stream_ref.1, bf16[3,128,6144]{2,1,0:T(8,128)(2,1)} %bitcast.2, f32[1,6144]{1,0:T(1,128)} %bitcast.3, ...), custom_call_target="tpu_custom_call" | custom-call | flops 10499999744 | bytes 12000000 | tf_op jit(solution)/shard_map/pallas_call | solution.py:525
  101.7 0.7 copy.11
  102.4 0.9 copy.12

commit v7 on v6

--- a/solution.py
+++ b/solution.py
@@ -426,6 +426,13 @@
         product = jnp.dot(xg[j], wb[j], preferred_element_type=F32)
         total[...] = product if start else total[...] + product
 
+    def expand_two(j, k):
+        total[...] += jnp.dot(
+            jnp.concatenate([xg[j], xg[k]], axis=1),
+            jnp.concatenate([wb[j], wb[k]], axis=0),
+            preferred_element_type=F32,
+        )
+
     go("xc", block(own), block(own), cp)
     go("wq2", wb.at[after, second], wb.at[after, second], yp)
     go.arrive("wf2")
@@ -492,8 +499,7 @@
     go.arrive_all("wy2", wb.at[opposite, second], yp)
     go.arrive_all("wq1", wb.at[before_opposite, second], yp)
     go.arrive("wp+b", "wp-b", "wq2")
-    expand(turn[0])
-    expand(turn[1])
+    expand_two(turn[0], turn[1])
     expand(turn[2])
     go.arrive_all("xf0", block(far_chip), xp)
     go("xcf0", block(far_chip), block(far_chip), cp)

time: 103 us -> 103 us (level)
  no operation moved by 1% of the time
where the time goes in v7:
time: 103 us
  Pallas kernels  101 us (98%)
  local copies, waits for them, and re-layouts  1.63 us (2%)
    pallas_call x1, Pallas kernels, body(): pl.pallas_call(kernel, out_shape=(pltpu.VMEM((ROWS, OWN), BF16), pltpu.VM...  101 us

profile of v7, /device:TPU:1, one launch (start us, length us, event | category | flops | bytes accessed | tf_op | source)
XLA Modules:
  0.0 103.3 jit_solution(13943526960857582813)
XLA Ops:
  0.6 101.1 %shard_map.86 = (bf16[512,384]{1,0:T(8,128)(2,1)S(1)}, bf16[512,768]{1,0:T(8,128)(2,1)S(1)}) custom-call(bf16[512,384]{1,0:T(8,128)(2,1)} %q_ref.1, bf16[512,384]{1,0:T(8,128)(2,1)} %k_ref.1, bf16[512,384]{1,0:T(8,128)(2,1)} %v_ref.1, bf16[512,384]{1,0:T(8,128)(2,1)} %stream_ref.1, bf16[3,128,6144]{2,1,0:T(8,128)(2,1)} %bitcast.2, f32[1,6144]{1,0:T(1,128)} %bitcast.3, ...), custom_call_target="tpu_custom_call" | custom-call | flops 10499999744 | bytes 12000000 | tf_op jit(solution)/shard_map/pallas_call | solution.py:531
  101.7 0.7 copy.11
  102.4 0.9 copy.12
